TPU v7x, 32 devices: a whole 2x2x4 slice. The times are simulated.
32 devices in a mesh: rows: 8 (over z, x), seq: 4 (over y, core).
Axes of the slice: x: 2, y: 2, z: 4, core: 2. Of those that a mesh axis runs over, the one named last changes fastest.
Arguments:
- tokens: bfloat16 [96, 512, 768], P('rows', 'seq'), may hold values from -6 to 6
- seg_lengths: int32 [96, 6], P('rows'), may hold values from 1 to 256, 512 in all within a row
- w_query: bfloat16 [768, 768], replicated, may hold values from -0.25 to 0.25
- w_key: bfloat16 [768, 768], replicated, may hold values from -0.25 to 0.25
- w_value: bfloat16 [768, 768], replicated, may hold values from -0.21875 to 0.21875
- w_output: bfloat16 [768, 768], replicated, may hold values from -0.625 to 0.625
- w_inner: bfloat16 [768, 3072], replicated, may hold values from -0.21875 to 0.21875
- w_outer: bfloat16 [3072, 768], replicated, may hold values from -0.1875 to 0.1875
- gain_attn: bfloat16 [768], replicated, may hold values from 0.099609375 to 1.8984375
- gain_ffn: bfloat16 [768], replicated, may hold values from 0.099609375 to 1.8984375
- bucket_bias_table: bfloat16 [32, 12], replicated, may hold values from -4 to 4
- cotangent: bfloat16 [96, 512, 768], P('rows', 'seq'), may hold values from -6 to 6
Outputs:
- out_tokens: bfloat16 [96, 512, 768], P('rows', 'seq')
- grad_tokens: bfloat16 [96, 512, 768], P('rows', 'seq')
- grad_query: float32 [768, 768], replicated
- grad_key: float32 [768, 768], replicated
- grad_value: float32 [768, 768], replicated
- grad_output: float32 [768, 768], replicated
- grad_inner: float32 [768, 3072], replicated
- grad_outer: float32 [3072, 768], replicated
- grad_gain_attn: float32 [768], replicated
- grad_gain_ffn: float32 [768], replicated
- grad_table: float32 [32, 12], replicated
Inputs may be any that keep to these rules, and one draw needn't show every extreme that they name: `seg_lengths`: each row's 6 entries sum to 512; the last is the row's padding; the largest entry of each row is 256.
All inputs are finite; a program needn't handle non-finite values.
Results may differ from a plain program's by a relative error of at most 0.015.
The roundings to bfloat16 on the way count: a program that leaves them out, or rounds other values in their place, can miss the bound.
Values may be sent and summed in bfloat16 or wider, within the bound.
A program may use at most 384 MiB of HBM per device.

v0:
```python
import functools
import math

import jax
import jax.numpy as jnp
from jax import lax
from jax.experimental import pallas as pl
from jax.experimental.pallas import tpu as pltpu
from jax.sharding import PartitionSpec as P

EPSILON = 1e-06
THRESHOLDS = (12, 16, 23, 32, 46, 64, 91)
NEGATIVE = -1e30
BUCKETS = 32
GELU_SCALE = math.sqrt(2.0 / math.pi)
GELU_CUBIC = 0.044715
LOG2E = math.log2(math.e)
BLK = 128
QT = 256
HALF = 64
ONES_AT = 8
BF = jnp.bfloat16
F32 = jnp.float32
TOK = 512
TILE_TOK = 256
MESH = pl.DeviceIdType.MESH
CH_ROWS, CH_COLS = 768, 256
SUM_STEPS = ((1,), (2,), (3,), (4,))
GIVE_STEPS = ((5,), (6,), (7,), (8,), (9,))
GIVE_LAG = 3
EARLY = 6
SWAPS = 12
SEQ = 4
SEND_SLOTS = 8
BOTH_STEPS = ((1,), (2,), (3,), (4, 5), (6,), (7,), (8,), (9,))
REST_LAG = 2


def bucket_of(offsets, bucket_count):
    distance = jnp.abs(offsets)
    levels = 8 + sum(((distance >= threshold).astype(jnp.int32) for threshold in THRESHOLDS))
    return jnp.where(offsets > 0, bucket_count // 2, 0) + jnp.where(distance < 8, distance, levels)


def segment_ids(seg_lengths, row_len):
    order = jnp.arange(seg_lengths.shape[1])
    ends = jnp.sum(
        jnp.where(order[None, :, None] <= order[None, None, :], seg_lengths[:, :, None], 0), axis=1
    )
    positions = jnp.arange(row_len, dtype=jnp.int32)
    return jnp.sum((positions[None, :, None] >= ends[:, None, :]).astype(jnp.int32), axis=2)


def gelu_both(x):
    square = x * x
    tangent = jnp.tanh(x * (GELU_SCALE + GELU_SCALE * GELU_CUBIC * square))
    upper = 0.5 * tangent + 0.5
    slope = upper + (0.5 * x) * (1.0 - tangent * tangent) * (
        GELU_SCALE + 3.0 * GELU_SCALE * GELU_CUBIC * square
    )
    return x * upper, slope


def apply_rms_scaling(values_in, gain_row):
    inverse = lax.rsqrt(jnp.mean(values_in * values_in, axis=-1, keepdims=True) + EPSILON)
    return (values_in * inverse * gain_row, inverse)


def norm_back(values_in, inverse, gain_row, grad_normed):
    weighted = grad_normed * gain_row
    inner_mean = jnp.mean(weighted * values_in, axis=-1, keepdims=True)
    grad_values = inverse * weighted - values_in * (inverse * inverse * inverse) * inner_mean
    grad_gain = jnp.sum(grad_normed * values_in * inverse, axis=0)
    return (grad_values, grad_gain)


def dot(a, b, ca, cb):
    return lax.dot_general(a, b, (((ca,), (cb,)), ((), ())), preferred_element_type=F32)


def halves(value, own, other, head):
    lane = lax.broadcasted_iota(jnp.int32, value.shape, 1)
    mine = (lane < HALF) if head == 0 else (lane >= HALF)
    return jnp.where(mine, value, other)


def stack_q(q_pair, features, head):
    scaled = q_pair[head * HALF : (head + 1) * HALF].astype(F32) * LOG2E
    high = scaled.astype(BF)
    low = (scaled - high.astype(F32)).astype(BF)
    zero = jnp.zeros_like(high)
    if head == 0:
        return jnp.concatenate([high, zero, low, features], axis=0)
    return jnp.concatenate([zero, high, features, low], axis=0)


def bias_tile(bias_ref, head, key_block, query_block, number, blocks):
    at = key_block - query_block + blocks - 1
    return jnp.concatenate([bias_ref[head, at - i] for i in range(number)], axis=1)


def attend_kernel(q_ref, k_ref, v_ref, fq_ref, fk_ref, bias_ref, *refs):
    if len(refs) > 2:
        away, mix_ref, stat_ref, near, *sems = refs
        swap = Exchange(away, near, *sems, True)
        now = pl.program_id(0) * pl.num_programs(1) + pl.program_id(1)

        @pl.when(now == 0)
        def _():
            swap.meet()
            swap.start(0)

        @pl.when(now == pl.num_programs(0) * pl.num_programs(1) - 1)
        def _():
            swap.wait(0)
    else:
        mix_ref, stat_ref = refs
    row_len = k_ref.shape[0]
    blocks = row_len // BLK
    keys, vals, features_q, features_k = k_ref[...], v_ref[...], fq_ref[0], fk_ref[0]
    q_pair = q_ref[...].T
    lane = lax.broadcasted_iota(jnp.int32, (row_len, BLK), 1)
    ones = jnp.ones_like(vals)
    queries = [stack_q(q_pair, features_q, h) for h in range(2)]
    keys_all = [jnp.concatenate([keys, halves(keys, None, features_k, h)], axis=1) for h in range(2)]
    values = [halves(vals, None, ones, h) for h in range(2)]
    mixed, stats = [], []
    for h in range(2):
        raw = dot(keys_all[h], queries[h], 1, 0)
        scores = [
            raw[b * BLK : (b + 1) * BLK] + bias_tile(bias_ref, h, b, 0, blocks, blocks)
            for b in range(blocks)
        ]
        top = functools.reduce(jnp.maximum, scores)
        top = jnp.max(top, axis=0, keepdims=True)
        probs = jnp.concatenate([jnp.exp2(s - top).astype(BF) for s in scores], axis=0)
        summed = dot(probs, values[h], 0, 0)
        at = HALF if h == 0 else 0
        total = summed[:, at : at + 1]
        mixed.append(summed * (1.0 / total))
        stats.append(top)
        stats.append(total)
    mix_ref[...] = jnp.where(lane < HALF, mixed[0], mixed[1]).astype(BF)
    totals = jnp.where(lane == 0, stats[1], stats[3]).T
    for h in range(2):
        stat_ref[0, 0, h : h + 1] = stats[2 * h] + jnp.log2(totals[h : h + 1])


def three(row):
    one = row.astype(BF)
    rest = row - one.astype(F32)
    two = rest.astype(BF)
    return one, two, (rest - two.astype(F32)).astype(BF)


def feature_rows(base, row):
    parts = three(row)
    at = lax.broadcasted_iota(jnp.int32, base.shape, 0)
    out = base.astype(F32)
    for i, part in enumerate(parts):
        out = jnp.where(at == ONES_AT + i, part.astype(F32), out)
    return out.astype(BF)


def block_buckets(at, blocks):
    ahead = (at - blocks + 1) * BLK
    low, high = ahead - BLK + 1, ahead + BLK - 1
    if low >= THRESHOLDS[-1] or high <= -THRESHOLDS[-1]:
        return BUCKETS - 1 if low > 0 else BUCKETS // 2 - 1, None, ()
    row = lax.broadcasted_iota(jnp.int32, (BLK, BLK), 0)
    lane = lax.broadcasted_iota(jnp.int32, (BLK, BLK), 1)
    first = BUCKETS // 2 if low > 0 else 0
    last = BUCKETS // 2 if high <= 0 else BUCKETS
    return None, bucket_of(ahead + row - lane, BUCKETS), range(first, last)


def bias_blocks(table_ref, bias_ref):
    heads, number = bias_ref.shape[:2]
    for at in range(number):
        one, bucket, some = block_buckets(at, (number + 1) // 2)

        def head_blocks(h, _):
            if one is not None:
                bias_ref[h, at] = jnp.full((BLK, BLK), table_ref[one, h] * LOG2E, F32)
                return 0
            value = jnp.zeros((BLK, BLK), F32)
            for b in some:
                value = jnp.where(bucket == b, table_ref[b, h] * LOG2E, value)
            bias_ref[h, at] = value
            return 0

        lax.fori_loop(0, heads, head_blocks, 0)


def bucket_sums(acc_ref, head, blocks):
    sums = BUCKETS * [jnp.zeros((1, BLK), F32)]
    for at in range(2 * blocks - 1):
        value = acc_ref[head, at]
        one, bucket, some = block_buckets(at, blocks)
        if one is not None:
            sums[one] = sums[one] + jnp.sum(value, axis=0, keepdims=True)
        for b in some:
            picked = jnp.sum(jnp.where(bucket == b, value, 0.0), axis=0, keepdims=True)
            sums[b] = sums[b] + picked
    return jnp.concatenate(sums, axis=0)


def attend_back_kernel(
    depth, q_ref, k_ref, v_ref, wp_ref, gb_ref, mix_ref, stat_ref, fq_ref, fk_ref, bias_ref, *refs
):
    if depth:
        share, done, dq_ref, dk_ref, dv_ref, table_ref, gi_ref, go_ref, out_ref = refs[:9]
        acc_ref, dk_sum, dv_sum, *sems = refs[9:15]
        swap = Exchange(done, out_ref, *sems, False, SWAPS)
        giving = Summing(
            depth, share, give_refs=refs[15:], targets=(gi_ref, go_ref), turned=True,
            given=(share.shape[0] // 2 - gi_ref.shape[1] // CH_COLS, share.shape[0] // 2),
        )
        now = pl.program_id(0) * pl.num_programs(1) + pl.program_id(1)

        @pl.when(now == 0)
        def _():
            giving.meet()

        @pl.when(now < SWAPS)
        def _():
            swap.start(now)

        giving.tick(now + giving.given[0] + GIVE_LAG, GIVE_STEPS, GIVE_LAG)
    else:
        dq_ref, dk_ref, dv_ref, table_ref, acc_ref, dk_sum, dv_sum = refs
    row_len = k_ref.shape[0]
    blocks = row_len // BLK
    keys, vals, features_k = k_ref[...], v_ref[...], fk_ref[0]
    k_flat = keys.T
    do_pair = dot(wp_ref[...], gb_ref[...], 1, 1).astype(BF)
    q_rows, do_rows = q_ref[...], do_pair.T
    q_pair, mix_pair = q_rows.T, mix_ref[...].T
    zero_rows = jnp.zeros((row_len, BLK), BF)

    @pl.when(pl.program_id(1) == 0)
    def _():
        acc_ref[...] = jnp.zeros_like(acc_ref)

    for head in range(2):
        span = slice(head * HALF, (head + 1) * HALF)
        do_head = do_pair[span]
        delta = jnp.sum(do_head.astype(F32) * mix_pair[span].astype(F32), axis=0, keepdims=True)
        zeros = jnp.zeros((HALF, row_len), BF)
        q_all = stack_q(q_pair, feature_rows(fq_ref[0], -stat_ref[0, 0, head : head + 1]), head)
        k_all = jnp.concatenate([keys, halves(keys, None, features_k, head)], axis=1)
        v_all = halves(vals, None, features_k, head)
        back = feature_rows(zeros, -delta)
        do_all = jnp.concatenate([do_head, back] if head == 0 else [back, do_head], axis=0)
        q_own = halves(q_rows, None, zero_rows, head)
        do_own = halves(do_rows, None, zero_rows, head)
        for tile in range(row_len // QT):
            cut = slice(tile * QT, (tile + 1) * QT)
            raw = dot(k_all, q_all[:, cut], 1, 0)
            grad_probs = dot(v_all, do_all[:, cut], 1, 0)
            probs_list, grads_list = [], []
            sums = {}
            for b in range(blocks):
                part = slice(b * BLK, (b + 1) * BLK)
                probs = jnp.exp2(raw[part] + bias_tile(bias_ref, head, b, tile * (QT // BLK), QT // BLK, blocks))
                grads = probs * grad_probs[part]
                probs_list.append(probs.astype(BF))
                grads_list.append(grads.astype(BF))
                for i in range(QT // BLK):
                    at = b - tile * (QT // BLK) - i + blocks - 1
                    piece = grads[:, i * BLK : (i + 1) * BLK]
                    sums[at] = sums[at] + piece if at in sums else piece
            for at, piece in sums.items():
                acc_ref[head, at] += piece
            probs_low = jnp.concatenate(probs_list, axis=0)
            grads_low = jnp.concatenate(grads_list, axis=0)
            dv_new = dot(probs_low, do_own[cut], 1, 0)
            dk_new = dot(grads_low, q_own[cut], 1, 0)
            if head == 0 and tile == 0:
                dv_sum[...] = dv_new
                dk_sum[...] = dk_new
            else:
                dv_sum[...] += dv_new
                dk_sum[...] += dk_new
            dq_ref[span, cut] = dot(k_flat[span], grads_low, 1, 0).astype(BF)
    dk_ref[...] = dk_sum[...].astype(BF)
    dv_ref[...] = dv_sum[...].astype(BF)

    @pl.when(pl.program_id(1) == pl.num_programs(1) - 1)
    def _():
        for head in range(2):
            table_ref[head] = bucket_sums(acc_ref, head, blocks)

    if depth:
        steps = pl.num_programs(0) * pl.num_programs(1)

        @pl.when(now == steps - 1)
        def _():
            giving.drain(steps + giving.given[0] + GIVE_LAG, GIVE_STEPS, GIVE_LAG)
            giving.finish()
            swap.finish()


def specs(row_len):
    flat = pl.BlockSpec((BLK, row_len), lambda g, r: (g, r))
    rows = pl.BlockSpec((row_len, BLK), lambda g, r: (r, g))
    stat = pl.BlockSpec((1, 1, 2, row_len), lambda g, r: (r, g, 0, 0))
    fq = pl.BlockSpec((1, HALF, row_len), lambda g, r: (r, 0, 0))
    fk = pl.BlockSpec((1, row_len, BLK), lambda g, r: (r, 0, 0))
    blocks = 2 * (row_len // BLK) - 1
    bias = pl.BlockSpec((2, blocks, BLK, BLK), lambda g, r: (g, 0, 0, 0))
    return flat, rows, stat, fq, fk, bias


def attend(q_rows, k_rows, v_rows, fq, fk, bias, row_len, away=None):
    count, width = q_rows.shape
    flat, rows, stat, fqs, fks, biass = specs(row_len)
    pairs, row_count = width // BLK, count // row_len
    anywhere = pl.BlockSpec(memory_space=pl.ANY)
    extra, near, scratch, params = (), [], [], {}
    if away is not None:
        extra, near = (away,), [jax.ShapeDtypeStruct((row_count, row_len, width), BF)]
        scratch, params = Exchange.scratch(), dict(collective_id=5, has_side_effects=True)
    return pl.pallas_call(
        attend_kernel,
        grid=(pairs, row_count),
        in_specs=[rows, rows, rows, fqs, fks, biass] + [anywhere] * len(extra),
        out_specs=[rows, stat] + [anywhere] * len(near),
        out_shape=[
            jax.ShapeDtypeStruct((count, width), BF),
            jax.ShapeDtypeStruct((row_count, pairs, 2, row_len), F32),
        ] + near,
        scratch_shapes=scratch,
        compiler_params=pltpu.CompilerParams(vmem_limit_bytes=48 << 20, **params),
        cost_estimate=pl.CostEstimate(
            flops=4 * 4 * width * count * row_len,
            bytes_accessed=8 * width * count,
            transcendentals=0,
        ),
    )(q_rows, k_rows, v_rows, fq, fk, bias, *extra)


def attend_back(q_rows, k_rows, v_rows, wp, gb, mix, stat_in, fq, fk, bias, row_len, gives):
    count, width = q_rows.shape
    flat, rows, stat, fqs, fks, biass = specs(row_len)
    pairs, row_count = width // BLK, count // row_len
    anywhere = pl.BlockSpec(memory_space=pl.ANY)
    depth, extra, extra_in, extra_out, scratch, params = 0, (), [], [], [], {}
    if gives is not None:
        share, depth, early, done = gives
        shapes = [(width, share.shape[0] // 2 * CH_COLS - early), (share.shape[0] // 2 * CH_COLS - early, width)]
        done = done.reshape(row_count, row_len, width)
        extra, extra_in = (share, done), [pl.BlockSpec(share.shape, lambda g, r: (0, 0, 0)), anywhere]
        extra_out = [jax.ShapeDtypeStruct(shape, BF) for shape in shapes]
        extra_out += [jax.ShapeDtypeStruct((row_count * SEQ, row_len // SEQ, width), BF)]
        scratch = Exchange.scratch(SWAPS) + Summing.give_scratch(share.shape[0], depth, True)
        params = dict(collective_id=3, has_side_effects=True)
    return pl.pallas_call(
        functools.partial(attend_back_kernel, depth),
        grid=(pairs, row_count),
        in_specs=[
            rows, rows, rows, pl.BlockSpec((BLK, width), lambda g, r: (g, 0)),
            pl.BlockSpec((row_len, width), lambda g, r: (r, 0)), rows, stat, fqs, fks, biass,
        ] + extra_in,
        out_specs=[flat, rows, rows, pl.BlockSpec((2, BUCKETS, BLK), lambda g, r: (g, 0, 0))]
        + [anywhere] * len(extra_out),
        out_shape=[
            jax.ShapeDtypeStruct((width, count), BF),
            jax.ShapeDtypeStruct((count, width), BF),
            jax.ShapeDtypeStruct((count, width), BF),
            jax.ShapeDtypeStruct((2 * pairs, BUCKETS, BLK), F32),
        ] + extra_out,
        scratch_shapes=[pltpu.VMEM((2,) + bias.shape[1:], F32)]
        + [pltpu.VMEM((row_len, BLK), F32)] * 2
        + scratch,
        compiler_params=pltpu.CompilerParams(vmem_limit_bytes=48 << 20, **params),
        cost_estimate=pl.CostEstimate(
            flops=10 * 4 * width * count * row_len,
            bytes_accessed=16 * width * count,
            transcendentals=0,
        ),
    )(q_rows, k_rows, v_rows, wp, gb, mix, stat_in, fq, fk, bias, *extra)


class Place:
    def __init__(self):
        self.r, self.s = lax.axis_index("rows"), lax.axis_index("seq")
        self.x, self.z = lax.rem(self.r, 2), self.r // 2
        self.core, self.y = lax.rem(self.s, 2), self.s // 2

    def at(self, x=None, y=None, core=None, z=None):
        x = self.x if x is None else x
        y = self.y if y is None else y
        core = self.core if core is None else core
        z = self.z if z is None else z
        return (z * 2 + x, y * 2 + core)


def spans(base, size, step=16):
    return pl.ds(pl.multiple_of(base, step), size)


class Exchange:
    def __init__(self, src, dst, send, recv, keep, to_rows, parts=1):
        self.src, self.dst, self.send, self.recv, self.keep, self.to_rows = src, dst, send, recv, keep, to_rows
        pieces, rows = (src, dst) if to_rows else (dst, src)
        self.mine, self.piece, self.parts = rows.shape[0], pieces.shape[1], parts
        self.r, self.s = lax.axis_index("rows"), lax.axis_index("seq")

    @staticmethod
    def scratch(parts=1):
        dma = pltpu.SemaphoreType.DMA
        return [dma((parts, SEQ - 1)), dma((parts, SEQ - 1)), dma((parts,))]

    def meet(self):
        barrier = pltpu.get_barrier_semaphore()
        for k in range(1, SEQ):
            place = (self.r, lax.rem(self.s + k, SEQ))
            pl.semaphore_signal(barrier, inc=1, device_id=place, device_id_type=MESH)
        pl.semaphore_wait(barrier, SEQ - 1)

    def ends(self, part, peer):
        if self.parts <= self.mine:
            size, long = self.mine // self.parts, self.piece
            row, at = part * size, 0
        else:
            cuts = self.parts // self.mine
            size, long = 1, self.piece // cuts
            row, at = part // cuts, lax.rem(part, cuts) * long
        if self.to_rows:
            return (self.src.at[pl.ds(peer * self.mine + row, size), spans(at, long)],
                    self.dst.at[pl.ds(row, size), spans(self.s * self.piece + at, long)])
        return (self.src.at[pl.ds(row, size), spans(peer * self.piece + at, long)],
                self.dst.at[pl.ds(self.s * self.mine + row, size), spans(at, long)])

    def copies(self, part):
        out = []
        for k in range(1, SEQ):
            peer = lax.rem(self.s + k, SEQ)
            src, dst = self.ends(part, peer)
            out.append(pltpu.make_async_remote_copy(
                src_ref=src, dst_ref=dst, send_sem=self.send.at[part, k - 1],
                recv_sem=self.recv.at[part, SEQ - 1 - k], device_id=(self.r, peer), device_id_type=MESH))
        src, dst = self.ends(part, self.s)
        return out, pltpu.make_async_copy(src, dst, self.keep.at[part])

    def start(self, part):
        away, here = self.copies(part)
        for d in away:
            d.start()
        here.start()

    def wait(self, part):
        away, here = self.copies(part)
        for d in away:
            d.wait()
        here.wait()

    def finish(self):
        def one(part, _):
            self.wait(part)
            return 0

        lax.fori_loop(0, self.parts, one, 0)


class Summing:
    def __init__(self, depth, share, sum_refs=None, give_refs=None, scale=1.0, targets=None, turned=False, mixed=True, given=None):
        if sum_refs is not None:
            (self.snd, self.got, self.own, self.got_one, self.got_two, self.got_z,
             self.send_sum, self.recv_sum, self.send_sum_z, self.recv_sum_z) = sum_refs
        if give_refs is not None:
            (self.gath, self.flip, self.sems,
             self.send_give, self.recv_give, self.send_give_z, self.recv_give_z) = give_refs
        self.summed = (0, share.shape[0] // 2)
        self.given = self.summed if given is None else given
        self.share, self.chunks, self.targets, self.turned = share, share.shape[0], targets, turned
        self.depth, self.scale, self.mixed = depth, scale, mixed
        self.me = Place()
        self.w = CH_COLS // 2
        self.half, self.quarter = CH_ROWS // 2, CH_ROWS // 4
        self.piece = CH_ROWS // (4 * depth)

    @staticmethod
    def sum_scratch(chunks, depth):
        w, piece = CH_COLS // 2, CH_ROWS // (4 * depth)
        dma = pltpu.SemaphoreType.DMA
        return [
            pltpu.VMEM((SEND_SLOTS, CH_ROWS, w), BF),
            pltpu.VMEM((chunks, CH_ROWS, w), BF),
            pltpu.VMEM((chunks, CH_ROWS, w), BF),
            pltpu.VMEM((chunks, CH_ROWS // 2, w), BF),
            pltpu.VMEM((chunks, CH_ROWS // 4, w), BF),
            pltpu.VMEM((chunks, depth - 1, piece, w), BF),
            dma((3, chunks)), dma((3, chunks)),
            dma((chunks, depth - 1)), dma((chunks, depth - 1)),
        ]

    @staticmethod
    def give_scratch(chunks, depth, turned):
        dma = pltpu.SemaphoreType.DMA
        return [
            pltpu.VMEM((chunks, 2, CH_ROWS, CH_COLS // 2), BF),
            pltpu.VMEM((2, CH_COLS, CH_ROWS) if turned else (1, 16, 128), BF),
            dma((2, chunks)),
            dma((3, chunks)), dma((3, chunks)),
            dma((chunks, depth - 1)), dma((chunks, depth - 1)),
        ]

    @staticmethod
    def share_shape(chunks, depth):
        return (chunks, CH_ROWS // (4 * depth), CH_COLS // 2)

    def meet(self):
        me = self.me
        barrier = pltpu.get_barrier_semaphore()
        others = [me.at(x=1 - me.x)] + [(me.r, lax.rem(me.s + k, SEQ)) for k in range(1, SEQ)]
        others += [me.at(z=lax.rem(me.z + k, self.depth)) for k in range(1, self.depth)]
        for place in others:
            pl.semaphore_signal(barrier, inc=1, device_id=place, device_id_type=MESH)
        pl.semaphore_wait(barrier, len(others))

    def copy(self, src, dst, stage, c, place):
        if stage < 3:
            send, recv = self.send_sum.at[stage, c], self.recv_sum.at[stage, c]
        else:
            send, recv = self.send_give.at[stage - 3, c], self.recv_give.at[stage - 3, c]
        return pltpu.make_async_remote_copy(
            src_ref=src, dst_ref=dst, send_sem=send, recv_sem=recv, device_id=place, device_id_type=MESH)

    def part(self, c, start, size):
        return self.gath.at[c, self.me.core, spans(start, size)]

    def order(self, c):
        me, odd = self.me, lax.rem(c, 2) if self.mixed else 0
        one = me.x + odd * (me.y - me.x)
        two = me.y + odd * (me.x - me.y)
        x_there, y_there = 1 - 2 * me.x, 2 - 4 * me.y
        first = (me.r + (1 - odd) * x_there, me.s + odd * y_there)
        second = (me.r + odd * x_there, me.s + (1 - odd) * y_there)
        return one, two, first, second

    def put(self, c, value):
        left, right = value[:, : self.w].astype(BF), value[:, self.w :].astype(BF)
        first = self.me.core == 0
        self.own[c] = jnp.where(first, left, right)
        self.snd[lax.rem(c, SEND_SLOTS)] = jnp.where(first, right, left)
        self.step_core(c).start()

    def step_core(self, c):
        return self.copy(self.snd.at[lax.rem(c, SEND_SLOTS)], self.got.at[c], 0, c, self.me.at(core=1 - self.me.core))

    def step_one(self, c):
        one, _, place, _ = self.order(c)
        return self.copy(self.own.at[c, spans((1 - one) * self.half, self.half)], self.got_one.at[c], 1, c, place)

    def step_two(self, c):
        one, two, _, place = self.order(c)
        part = spans(one * self.half + (1 - two) * self.quarter, self.quarter)
        return self.copy(self.own.at[c, part], self.got_two.at[c], 2, c, place)

    def base(self, c):
        one, two, _, _ = self.order(c)
        return one * self.half + two * self.quarter

    def step_z(self, c, k):
        to = lax.rem(self.me.z + k, self.depth)
        return pltpu.make_async_remote_copy(
            src_ref=self.own.at[c, spans(self.base(c) + to * self.piece, self.piece)],
            dst_ref=self.got_z.at[c, self.depth - 1 - k],
            send_sem=self.send_sum_z.at[c, k - 1], recv_sem=self.recv_sum_z.at[c, self.depth - 1 - k],
            device_id=self.me.at(z=to), device_id_type=MESH)

    def mine(self, c):
        return self.part(c, self.base(c) + self.me.z * self.piece, self.piece)

    def give_z(self, c, k):
        return pltpu.make_async_remote_copy(
            src_ref=self.mine(c), dst_ref=self.mine(c),
            send_sem=self.send_give_z.at[c, k - 1], recv_sem=self.recv_give_z.at[c, self.depth - 1 - k],
            device_id=self.me.at(z=lax.rem(self.me.z + k, self.depth)), device_id_type=MESH)

    def give_two(self, c):
        part = self.part(c, self.base(c), self.quarter)
        return self.copy(part, part, 3, c, self.order(c)[3])

    def give_one(self, c):
        one, _, place, _ = self.order(c)
        part = self.part(c, one * self.half, self.half)
        return self.copy(part, part, 4, c, place)

    def give_core(self, c):
        part = self.part(c, 0, CH_ROWS)
        return self.copy(part, part, 5, c, self.me.at(core=1 - self.me.core))

    def leave(self, c, kind):
        if len(self.targets) == 1:
            array, at = self.targets[0], c * CH_COLS
        else:
            array, at = self.targets[kind], (c // 2 - self.given[0]) * CH_COLS
        if self.turned and kind == 1:
            flip = self.flip.at[lax.rem(c // 2, 2)]
            return [pltpu.make_async_copy(flip, array.at[spans(at, CH_COLS, CH_COLS)], self.sems.at[0, c])]
        return [
            pltpu.make_async_copy(
                self.gath.at[c, i], array.at[:, spans(at + i * self.w, self.w, 128)], self.sems.at[i, c])
            for i in range(2)
        ]

    def add(self, c, start, size, from_ref):
        part = spans(start, size)
        self.own[c, part] = (self.own[c, part].astype(F32) + from_ref[c].astype(F32)).astype(BF)

    def run(self, stage, c, kind):
        depth = self.depth
        if stage == 1:
            self.step_core(c).wait()
            self.add(c, 0, CH_ROWS, self.got)
            self.step_one(c).start()
        if stage == 2:
            self.step_one(c).wait_recv()
            self.add(c, self.order(c)[0] * self.half, self.half, self.got_one)
            self.step_two(c).start()
        if stage == 3:
            self.step_two(c).wait_recv()
            self.add(c, self.base(c), self.quarter, self.got_two)
            for k in range(1, depth):
                self.step_z(c, k).start()
        if stage == 4:
            for k in range(1, depth):
                self.step_z(c, k).wait_recv()
            total = self.own[c, spans(self.base(c) + self.me.z * self.piece, self.piece)].astype(F32)
            for k in range(depth - 1):
                total = total + self.got_z[c, k].astype(F32)
            self.share[c] = (total * self.scale).astype(BF)
            for d in (self.step_one(c), self.step_two(c)):
                d.wait_send()
            for k in range(1, depth):
                self.step_z(c, k).wait_send()
        if stage == 5:
            self.gath[c, self.me.core, spans(self.base(c) + self.me.z * self.piece, self.piece)] = self.share[c]
            for k in range(1, depth):
                self.give_z(c, k).start()
        if stage == 6:
            for k in range(1, depth):
                self.give_z(c, k).wait_recv()
            self.give_two(c).start()
        if stage == 7:
            self.give_two(c).wait_recv()
            self.give_one(c).start()
        if stage == 8:
            self.give_one(c).wait_recv()
            self.give_core(c).start()
        if stage == 9:
            self.give_core(c).wait_recv()
            if self.turned and kind == 1:

                @pl.when(c // 2 >= self.given[0] + 2)
                def _():
                    for d in self.leave(c - 4, kind):
                        d.wait()

                slot = lax.rem(c // 2, 2)
                for i in range(2):
                    self.flip[slot, i * self.w : (i + 1) * self.w] = self.gath[c, i].T
            for d in self.leave(c, kind):
                d.start()
            for d in (self.give_two, self.give_one, self.give_core):
                d(c).wait_send()
            for k in range(1, depth):
                self.give_z(c, k).wait_send()

    def tick(self, t, steps, lag):
        for at in range(len(steps), 0, -1):
            p = t - at * lag
            for stage in steps[at - 1]:
                low, high = self.summed if stage < 5 else self.given

                @pl.when((p >= low) & (p < high))
                def _():
                    for kind in range(2):
                        self.run(stage, 2 * p + kind, kind)

    def drain(self, start, steps, lag):
        def one(t, _):
            self.tick(t, steps, lag)
            return 0

        last = 0
        for at in range(len(steps), 0, -1):
            for stage in steps[at - 1]:
                last = max(last, (self.summed if stage < 5 else self.given)[1] + at * lag)
        lax.fori_loop(start, last, one, 0)

    def finish(self):
        def one(c, kind):
            for d in self.leave(c, kind):
                d.wait()

        def pair(p, _):
            one(2 * p, 0)
            if not self.turned:
                one(2 * p + 1, 1)
            return 0

        low, high = self.given
        lax.fori_loop(low, high, pair, 0)
        if self.turned:
            for p in range(max(low, high - 2), high):
                one(2 * p + 1, 1)


def before_kernel(
    fused, tok, gain, wq, wk, wv, table, normed_ref, flat_ref, q_ref, k_ref, v_ref, bias_ref, *refs
):
    if fused:
        tok_ref, rows, *sems = refs
        swap = Exchange(tok, rows, *sems, True, rows.shape[0])
        m = pl.program_id(0)

        @pl.when(m == 0)
        def _():
            swap.meet()
            for part in range(rows.shape[0]):
                swap.start(part)

    @pl.when(pl.program_id(0) == 0)
    def _():
        bias_blocks(table, bias_ref)

    if fused:
        swap.wait(m)
        own = rows[m]
        tok_ref[...] = own
        wide = own.astype(F32)
    else:
        wide = tok[...].astype(F32)
    normed = apply_rms_scaling(wide, gain[...])[0].astype(BF)
    normed_ref[...] = normed
    flat_ref[...] = normed.T
    q_ref[...] = dot(normed, wq[...], 1, 0).astype(BF)
    k_ref[...] = dot(normed, wk[...], 1, 0).astype(BF)
    v_ref[...] = dot(normed, wv[...], 1, 0).astype(BF)


def tall(width):
    return pl.BlockSpec((TOK, width), lambda m: (m, 0))


def broad(width):
    return pl.BlockSpec((width, TOK), lambda m: (0, m))


def whole(array):
    return pl.BlockSpec(array.shape, lambda m: (0,) * array.ndim)


def plain_call(kernel, count, ins, in_specs, outs, out_specs, flops, scratch=(), collective_id=None):
    params = {} if collective_id is None else dict(collective_id=collective_id, has_side_effects=True)
    return pl.pallas_call(
        kernel,
        grid=(count // TOK,),
        in_specs=in_specs,
        out_specs=out_specs,
        out_shape=[jax.ShapeDtypeStruct(shape, kind) for shape, kind in outs],
        scratch_shapes=list(scratch),
        compiler_params=pltpu.CompilerParams(vmem_limit_bytes=48 << 20, **params),
        cost_estimate=pl.CostEstimate(flops=flops, bytes_accessed=16 << 20, transcendentals=0),
    )(*ins)


def before(tok, gain, wq, wk, wv, table, mine, fused):
    width = tok.shape[-1]
    count = tok.size // width
    t, f = tall(width), broad(width)
    spec, more, scratch = t, [], []
    bias = (table.shape[1], 2 * (count // mine // BLK) - 1, BLK, BLK)
    if fused:
        spec = pl.BlockSpec(memory_space=pl.ANY)
        more = [((count, width), BF)]
        scratch = [pltpu.VMEM((mine, count // mine, width), BF)] + Exchange.scratch(mine)
    return plain_call(
        functools.partial(before_kernel, fused), count, (tok, gain, wq, wk, wv, table),
        [spec] + [whole(a) for a in (gain, wq, wk, wv)] + [pl.BlockSpec(memory_space=pltpu.SMEM)],
        [((count, width), BF), ((width, count), BF)] + [((count, width), BF)] * 3
        + [(bias, F32)] + more,
        [t, f, t, t, t] + [pl.BlockSpec(bias, lambda m: (0, 0, 0, 0))] + [t] * len(more), 6 * count * width * width, scratch, 4 if fused else None,
    )


def between_kernel(tok, mix, wo, gain, dy, hidden_ref, nt_ref, nt_flat_ref, dy_flat_ref, mix_flat_ref):
    hidden = tok[...].astype(F32) + dot(mix[...], wo[...], 1, 0)
    hidden_ref[...] = hidden
    normed = apply_rms_scaling(hidden, gain[...])[0].astype(BF)
    nt_ref[...] = normed
    nt_flat_ref[...] = normed.T
    dy_flat_ref[...] = dy[...].T
    mix_flat_ref[...] = mix[...].T


def between(tok, mix, wo, gain, dy):
    count, width = tok.shape
    t, f = tall(width), broad(width)
    return plain_call(
        between_kernel, count, (tok, mix, wo, gain, dy), [t, t, whole(wo), whole(gain), t],
        [((count, width), F32), ((count, width), BF)] + [((width, count), BF)] * 3,
        [t, t, f, f, f], 2 * count * width * width,
    )


def after_kernel(tok, gain, gh, dq, dk, dv, wq, wk, wv, grad_ref, gain_ref):
    wide = tok[...].astype(F32)
    _, inverse = apply_rms_scaling(wide, gain[...])
    grad_normed = (
        dot(dq[...].T, wq[...], 1, 1) + dot(dk[...], wk[...], 1, 1) + dot(dv[...], wv[...], 1, 1)
    )
    part, grad_gain = norm_back(wide, inverse, gain[...], grad_normed)
    grad_ref[...] = (gh[...] + part).astype(BF)

    @pl.when(pl.program_id(0) == 0)
    def _():
        gain_ref[...] = jnp.zeros_like(gain_ref)

    gain_ref[...] += grad_gain[None]


def after(tok, gain, gh, dq, dk, dv, wq, wk, wv):
    count, width = tok.shape
    t, f = tall(width), broad(width)
    return plain_call(
        after_kernel, count, (tok, gain, gh, dq, dk, dv, wq, wk, wv),
        [t, whole(gain), t, f, t, t, whole(wq), whole(wk), whole(wv)],
        [((count, width), BF), ((1, width), F32)], [t, whole(gain)], 6 * count * width * width,
    )


def ffn_kernel(depth, scale, nt, nt_flat, dy, dy_flat, gain, wi_hbm, wo_hbm, hidden_hbm,
               res_hbm, gh_hbm, gb_hbm, gain_ref, share, gi_ref, go_ref,
               out_acc, gnt_acc, wi_buf, wo_buf, act, gp, hid, res_buf, gb_buf, w_sem, h_sem, *refs):
    count, width = nt.shape
    tile = 2 * CH_COLS
    tiles = wi_hbm.shape[1] // tile
    parts = count // TOK
    given = gi_ref.shape[1] // CH_COLS
    summing = Summing(
        depth, share, refs[:10], refs[10:], scale, targets=(gi_ref, go_ref), turned=True, given=(0, given)
    )

    def weights(j):
        cut, slot = spans(j * tile, tile, tile), lax.rem(j, 2)
        return (
            pltpu.make_async_copy(wi_hbm.at[:, cut], wi_buf.at[slot], w_sem.at[0, slot]),
            pltpu.make_async_copy(wo_hbm.at[cut], wo_buf.at[slot], w_sem.at[1, slot]),
        )

    def hidden(m):
        return pltpu.make_async_copy(hidden_hbm.at[pl.ds(m * TOK, TOK)], hid, h_sem.at[0])

    for w in weights(0):
        w.start()
    hidden(0).start()
    out_acc[...] = jnp.zeros_like(out_acc)
    gnt_acc[...] = jnp.zeros_like(gnt_acc)
    summing.meet()

    def step(j, _):
        for w in weights(j):
            w.wait()

        @pl.when(j + 1 < tiles)
        def _():
            for w in weights(j + 1):
                w.start()

        slot = lax.rem(j, 2)
        wi, wo = wi_buf.at[slot], wo_buf.at[slot]
        for m in range(count // TILE_TOK):
            part = slice(m * TILE_TOK, (m + 1) * TILE_TOK)
            pre = dot(nt[part], wi[...], 1, 0)
            grad_active = dot(dy[part], wo[...], 1, 1)
            value, slope = gelu_both(pre)
            act[part] = value.astype(BF)
            gp[part] = (grad_active * slope).astype(BF)
        for h in range(2):
            cut = slice(h * CH_COLS, (h + 1) * CH_COLS)
            summing.put(4 * j + 2 * h, dot(nt_flat[...], gp[:, cut], 1, 0))
            summing.put(4 * j + 2 * h + 1, dot(dy_flat[...], act[:, cut], 1, 0))
            if h == 0:
                summing.tick(2 * j, BOTH_STEPS, 1)
        for m in range(count // TILE_TOK):
            part = slice(m * TILE_TOK, (m + 1) * TILE_TOK)
            out_acc[part] += dot(act[part], wo[...], 1, 0)
            gnt_acc[part] += dot(gp[part], wi[...], 1, 1)
        summing.tick(2 * j + 1, BOTH_STEPS, 1)
        return 0

    lax.fori_loop(0, tiles, step, 0)

    def outputs(m):
        rows = pl.ds(m * TOK, TOK)
        return (
            pltpu.make_async_copy(res_buf.at[m % 2], res_hbm.at[rows], h_sem.at[1 + m % 2]),
            pltpu.make_async_copy(gb_buf.at[m % 2], gb_hbm.at[rows], h_sem.at[3 + m % 2]),
            pltpu.make_async_copy(gnt_acc.at[rows], gh_hbm.at[rows], h_sem.at[5 + m % 2]),
        )

    total_gain = jnp.zeros((1, width), F32)
    gain_row = gain[...]
    for m in range(parts):
        summing.tick(2 * tiles + m, BOTH_STEPS, 1)
        rows = slice(m * TOK, (m + 1) * TOK)
        hidden(m).wait()
        if m >= 2:
            for d in outputs(m - 2):
                d.wait()
        value = hid[...]
        res_buf[m % 2] = (value + out_acc[rows]).astype(BF)
        _, inverse = apply_rms_scaling(value, gain_row)
        part, grad_gain = norm_back(value, inverse, gain_row, gnt_acc[rows])
        total_gain = total_gain + grad_gain[None]
        grad_hidden = dy[rows].astype(F32) + part
        gnt_acc[rows] = grad_hidden
        gb_buf[m % 2] = grad_hidden.astype(BF)
        if m + 1 < parts:
            hidden(m + 1).start()
        for d in outputs(m):
            d.start()
    gain_ref[...] = total_gain
    summing.drain(2 * tiles + parts, BOTH_STEPS, 1)
    summing.finish()
    for m in range(max(0, parts - 2), parts):
        for d in outputs(m):
            d.wait()


def ffn_summed(nt, nt_flat, dy, dy_flat, gain, w_inner, w_outer, hidden, scale, depth):
    count, width = nt.shape
    ff = w_inner.shape[1]
    chunks = 2 * ff // CH_COLS
    tile = 2 * CH_COLS
    vm = pl.BlockSpec(memory_space=pltpu.VMEM)
    anywhere = pl.BlockSpec(memory_space=pl.ANY)
    return pl.pallas_call(
        functools.partial(ffn_kernel, depth, scale),
        in_specs=[vm] * 5 + [anywhere] * 3,
        out_specs=[anywhere] * 3 + [vm] * 2 + [anywhere] * 2,
        out_shape=[
            jax.ShapeDtypeStruct((count, width), BF),
            jax.ShapeDtypeStruct((count, width), F32),
            jax.ShapeDtypeStruct((count, width), BF),
            jax.ShapeDtypeStruct((1, width), F32),
            jax.ShapeDtypeStruct(Summing.share_shape(chunks, depth), BF),
            jax.ShapeDtypeStruct((width, EARLY * CH_COLS), BF),
            jax.ShapeDtypeStruct((EARLY * CH_COLS, width), BF),
        ],
        scratch_shapes=[
            pltpu.VMEM((count, width), F32),
            pltpu.VMEM((count, width), F32),
            pltpu.VMEM((2, width, tile), BF),
            pltpu.VMEM((2, tile, width), BF),
            pltpu.VMEM((count, tile), BF),
            pltpu.VMEM((count, tile), BF),
            pltpu.VMEM((TOK, width), F32),
            pltpu.VMEM((2, TOK, width), BF),
            pltpu.VMEM((2, TOK, width), BF),
            pltpu.SemaphoreType.DMA((2, 2)),
            pltpu.SemaphoreType.DMA((7,)),
        ] + Summing.sum_scratch(chunks, depth) + Summing.give_scratch(2 * EARLY, depth, True),
        compiler_params=pltpu.CompilerParams(
            collective_id=1, has_side_effects=True, vmem_limit_bytes=62 << 20),
        cost_estimate=pl.CostEstimate(
            flops=12 * count * width * ff, bytes_accessed=40 << 20, transcendentals=0),
    )(nt, nt_flat, dy, dy_flat, gain, w_inner, w_outer, hidden)


def rest_kernel(depth, scale, *refs):
    sources, (small, done, out, out_ref) = refs[:6], refs[6:10]
    mix, gb, normed_flat, dq, dk, dv = held = refs[10:16]
    load_sem, share, *refs = refs[16:]
    width = normed_flat.shape[0]
    each = width // CH_COLS
    chunks = share.shape[0]
    loads = [pltpu.make_async_copy(a, b, load_sem.at[i]) for i, (a, b) in enumerate(zip(sources, held))]
    needs = (loads[:2], loads[2:4], loads[4:5], loads[5:])
    for d in loads:
        d.start()
    swap = Exchange(done, out_ref, *refs[:3], False, SWAPS)
    summing = Summing(depth, share, refs[3:13], refs[13:], scale, targets=(out,), mixed=False)
    summing.meet()

    def terms(which, cut):
        if which == 0:
            return dot(mix[...], gb[:, cut], 1, 0)
        if which == 1:
            return dot(normed_flat[...], dq[cut], 1, 1)
        return dot(normed_flat[...], (dk if which == 2 else dv)[:, cut], 1, 0)

    def step(p, _):
        for kind in range(2):
            c = 2 * p + kind
            for which in range(4):

                @pl.when(c // each == which)
                def _():
                    @pl.when(c == which * each)
                    def _():
                        for d in needs[which]:
                            d.wait()

                    cut = spans((c - which * each) * CH_COLS, CH_COLS, CH_COLS)
                    summing.put(c, terms(which, cut))

            @pl.when(c >= 4 * each)
            def _():
                summing.put(c, small[:, spans((c - 4 * each) * CH_COLS, CH_COLS, CH_COLS)])

        for i in range(2):

            @pl.when(2 * p + i < SWAPS)
            def _():
                swap.start(2 * p + i)

        summing.tick(p, BOTH_STEPS, REST_LAG)
        return 0

    lax.fori_loop(0, chunks // 2, step, 0)
    summing.drain(chunks // 2, BOTH_STEPS, REST_LAG)
    summing.finish()
    swap.finish()


def rest_summed(normed_flat, dq, dk, dv, mix, gb, small, done, scale, depth):
    width, count = normed_flat.shape
    chunks = (4 * width + small.shape[1]) // CH_COLS
    vm = pl.BlockSpec(memory_space=pltpu.VMEM)
    anywhere = pl.BlockSpec(memory_space=pl.ANY)
    mine, row_len, _ = done.shape
    sources = (mix, gb, normed_flat, dq, dk, dv)
    return pl.pallas_call(
        functools.partial(rest_kernel, depth, scale),
        in_specs=[anywhere] * 6 + [vm, anywhere],
        out_specs=[anywhere] * 2,
        out_shape=[
            jax.ShapeDtypeStruct((CH_ROWS, chunks * CH_COLS), BF),
            jax.ShapeDtypeStruct((mine * SEQ, row_len // SEQ, width), BF),
        ],
        scratch_shapes=[pltpu.VMEM(a.shape, BF) for a in sources]
        + [pltpu.SemaphoreType.DMA((6,)), pltpu.VMEM(Summing.share_shape(chunks, depth), BF)]
        + Exchange.scratch(SWAPS)
        + Summing.sum_scratch(chunks, depth)
        + Summing.give_scratch(chunks, depth, False),
        compiler_params=pltpu.CompilerParams(
            collective_id=2, has_side_effects=True, vmem_limit_bytes=60 << 20),
    )(*sources, small, done)


def reduce_plain(flat, scale):
    share = lax.psum_scatter(flat, ("rows", "seq"), scatter_dimension=0, tiled=True)
    share = (share.astype(F32) * scale).astype(BF)
    return lax.all_gather(share, ("rows", "seq"), axis=0, tiled=True)


def prepare(seg_lengths, mine, row_len):
    seg_count = seg_lengths.shape[1]
    lengths = lax.dynamic_slice_in_dim(seg_lengths, lax.axis_index("seq") * mine, mine, 0)
    seg = segment_ids(lengths, row_len)
    slots = jnp.arange(HALF, dtype=jnp.int32)
    fq = (seg[:, None, :] == slots[None, :, None]).astype(BF)
    fk_half = jnp.where(
        slots < seg_count,
        jnp.where(seg[:, :, None] != slots, NEGATIVE, 0.0),
        jnp.where((slots >= ONES_AT) & (slots < ONES_AT + 3), 1.0, 0.0),
    ).astype(BF)
    fk = jnp.concatenate([fk_half, fk_half], axis=2)
    return fq, fk


def per_device(
    tokens, seg_lengths, w_query, w_key, w_value, w_output, w_inner, w_outer,
    gain_attn, gain_ffn, bucket_bias_table, cotangent,
):
    rows_dev, piece_len, width = tokens.shape
    seq_parts = lax.axis_size("seq")
    row_len = piece_len * seq_parts
    mine = rows_dev // seq_parts
    count = mine * row_len
    gain_one = gain_attn.astype(F32)[None]
    gain_two = gain_ffn.astype(F32)[None]
    depth = lax.axis_size("rows") // 2
    scale = float(rows_dev * lax.axis_size("rows") * row_len) ** (-0.5)
    fused = seq_parts == 4 and CH_ROWS % (4 * depth * 16) == 0 and width == CH_ROWS

    def to_rows(array_in):
        out = lax.all_to_all(array_in, "seq", split_axis=0, concat_axis=1, tiled=True)
        return lax.optimization_barrier(out.reshape(count, width))

    def from_rows(array_in):
        return lax.all_to_all(
            array_in.reshape(mine, row_len, width), "seq", split_axis=1, concat_axis=0, tiled=True
        )

    fq, fk = prepare(seg_lengths, mine, row_len)
    tok = tokens if fused else to_rows(tokens)
    normed, normed_flat, q_rows, k_rows, v_rows, bias, *rows = before(
        tok, gain_one, w_query, w_key, w_value, bucket_bias_table.astype(F32), mine, fused
    )
    if fused:
        tok = rows[0]
    mix, stat, *near = attend(
        q_rows, k_rows, v_rows, fq, fk, bias, row_len, cotangent if fused else None
    )
    dy = near[0].reshape(count, width) if fused else to_rows(cotangent)
    hidden, nt, nt_flat, dy_flat, mix_flat = between(tok, mix, w_output, gain_two, dy)
    if fused:
        result, grad_hidden, branch, sum_two, share, *early = ffn_summed(
            nt, nt_flat, dy, dy_flat, gain_two, w_inner, w_outer, hidden, scale, depth
        )
        gives = (share, depth, early[0].shape[1], result)
    else:
        value, slope = gelu_both(dot(nt, w_inner, 1, 0))
        active = value.astype(BF)
        grad_pre = (dot(dy, w_outer, 1, 1) * slope).astype(BF)
        result = (hidden + dot(active, w_outer, 1, 0)).astype(BF)
        sum_outer, sum_inner = dot(active, dy, 0, 0), dot(grad_pre, nt, 0, 0)
        _, inverse = apply_rms_scaling(hidden, gain_two)
        part, sum_two = norm_back(hidden, inverse, gain_two, dot(grad_pre, w_inner, 1, 1))
        grad_hidden = dy.astype(F32) + part
        branch = grad_hidden.astype(BF)
        gives = None
    dq_flat, dk_rows, dv_rows, table, *given = attend_back(
        q_rows, k_rows, v_rows, w_output, branch, mix, stat, fq, fk, bias, row_len, gives
    )
    grad_input, sum_one = after(
        tok, gain_one, grad_hidden, dq_flat, dk_rows, dv_rows, w_query, w_key, w_value
    )
    sum_table = jnp.sum(table, axis=2).T
    small = jnp.concatenate([sum_one.reshape(-1), sum_two.reshape(-1), sum_table.reshape(-1)])
    if fused:
        small = jnp.pad(small, (0, -small.size % (CH_ROWS * BLK))).reshape(CH_ROWS, BLK)
        small = jnp.pad(small.astype(BF), ((0, 0), (0, 2 * CH_COLS - BLK)))
        total, grad_back = rest_summed(
            normed_flat, dq_flat, dk_rows, dv_rows, mix_flat, branch, small,
            grad_input.reshape(mine, row_len, width), scale, depth,
        )
        out_back = given[2]
        grad_inner = jnp.concatenate([early[0], given[0]], axis=1).astype(F32)
        grad_outer = jnp.concatenate([early[1], given[1]], axis=0).astype(F32)
        squares = [total[:, i * width : (i + 1) * width].astype(F32) for i in range(4)]
        rest = total[:, 4 * width : 4 * width + BLK].astype(F32).reshape(-1)
    else:
        devices = lax.axis_size("rows") * seq_parts
        small = jnp.pad(small, (0, -small.size % (16 * devices * width))).reshape(-1, width)
        parts = (
            dot(mix_flat, branch, 1, 0), dot(normed, dq_flat, 0, 1), dot(normed, dk_rows, 0, 0),
            dot(normed, dv_rows, 0, 0), small, sum_outer, sum_inner,
        )
        total = reduce_plain(jnp.concatenate([g.astype(BF) for g in parts]), scale).astype(F32)
        outs, at = [], 0
        for g in parts:
            outs.append(total[at : at + g.shape[0]])
            at += g.shape[0]
        squares, grad_outer, grad_inner = outs[:4], outs[5], outs[6].T
        rest = outs[4].reshape(-1)
        out_back, grad_back = from_rows(result), from_rows(grad_input)
    return (
        out_back,
        grad_back,
        squares[1],
        squares[2],
        squares[3],
        squares[0],
        grad_inner,
        grad_outer,
        rest[:width],
        rest[width : 2 * width],
        rest[2 * width : 2 * width + sum_table.size].reshape(sum_table.shape),
    )


def solution(mesh):
    tok = P("rows", "seq", None)
    in_specs = (tok, P("rows", None)) + (P(),) * 9 + (tok,)
    out_specs = (tok, tok) + (P(),) * 9
    return jax.shard_map(
        per_device, mesh=mesh, in_specs=in_specs, out_specs=out_specs, check_vma=False
    )
```

profile of v0, /device:TPU:1, one launch (start us, length us, event | category | flops | bytes accessed | tf_op | source)
XLA Modules:
  0.0 384.9 jit_solution(9579344565916910209)
XLA Ops:
  0.6 0.0 copy-start
  0.7 0.7 reshape.79.gain
  1.4 0.7 reshape.80.gain
  2.1 0.0 copy-done
  2.1 0.1 constant_dynamic-slice_fusion
  2.1 0.1 copy.38
  2.2 0.1 select_reduce_fusion
  2.3 0.1 convert_reduce_fusion
  2.4 0.8 copy.37.table
  3.2 0.3 select_convert_fusion
  3.5 0.2 pad_maximum_fusion.fk_ref
  3.8 0.0 copy-start.10
  3.8 1.3 copy-done.10
  5.0 1.3 copy-done.12
  6.3 1.3 copy-done.14
  7.6 36.2 %shard_map.203 = (bf16[1536,768]{1,0:T(8,128)(2,1)}, bf16[768,1536]{1,0:T(8,128)(2,1)}, bf16[1536,768]{1,0:T(8,128)(2,1)}, bf16[1536,768]{1,0:T(8,128)(2,1)}, bf...) custom-call(bf16[12,128,768]{2,1,0:T(8,128)(2,1)} %tok.1, ...), custom_call_target="tpu_custom_call" | custom-call | flops 5435817984 | bytes 16777216 | tf_op jit(solution)/shard_map/pallas_call | solution.py:760
  43.8 0.0 copy-start.6
  43.8 31.2 %shard_map.204 = (bf16[1536,768]{1,0:T(8,128)(2,1)S(1)}, f32[3,6,2,512]{3,2,1,0:T(2,128)S(1)}, bf16[3,512,768]{2,1,0:T(8,128)(2,1)S(1)}) custom-call(bf16[1536,768]{1,0:T(8,128)(2,1)} %get-tuple-element.43.q_ref, bf16[1536,768]{1,0:T(8,128)(2,1)} %get-tuple-element.44.k_ref, bf16[1536,768]{1,0:T(8,128)(2,1)} %get-tuple-element.45.v_ref, ...), custom_call_target="tpu_custom_call" | custom-call | flops 9663676416 | bytes 9437184 | tf_op jit(solution)/shard_map/pallas_call | solution.py:324
  75.0 0.0 copy-start.2
  75.0 1.4 copy-done.2
  76.4 1.4 copy-done.3
  77.8 0.0 copy-done.6
  77.8 8.9 %shard_map.205 = (f32[1536,768]{1,0:T(8,128)}, bf16[1536,768]{1,0:T(8,128)(2,1)S(1)}, bf16[768,1536]{1,0:T(8,128)(2,1)S(1)}, bf16[768,1536]{1,0:T(8,128)(2,1)}, bf16[768,1536]{1,0:T(8,128)(2,1)}) custom-call(bf16[1536,768]{1,0:T(8,128)(2,1)} %get-tuple-element.46.tok, bf16[1536,768]{1,0:T(8,128)(2,1)} %copy-done.2, bf16[768,768]{1,0:T(8,128)(2,1)S(1)} %copy-done.6, ...), custom_call_target="tpu_custom_call" | custom-call | flops 1811939328 | bytes 16777216 | tf_op jit(solution)/shard_map/pallas_call | solution.py:760
  86.7 1.4 copy-done.8
  88.1 1.4 copy-done.9
  89.5 102.1 %shard_map.206 = (bf16[1536,768]{1,0:T(8,128)(2,1)}, f32[1536,768]{1,0:T(8,128)}, bf16[1536,768]{1,0:T(8,128)(2,1)}, f32[1,768]{1,0:T(1,128)}, bf16[24,48,128]{2...) custom-call(bf16[1536,768]{1,0:T(8,128)(2,1)} %copy-done.8, bf16[768,1536]{1,0:T(8,128)(2,1)} %copy-done.9, ...), custom_call_target="tpu_custom_call" | custom-call | flops 43486543872 | bytes 41943040 | tf_op jit(solution)/shard_map/pallas_call | solution.py:943
  191.6 1.0 copy-done.16
  192.6 69.2 %shard_map.207 = (bf16[768,1536]{1,0:T(8,128)(2,1)S(1)}, bf16[1536,768]{1,0:T(8,128)(2,1)}, bf16[1536,768]{1,0:T(8,128)(2,1)}, f32[12,32,128]{2,1,0:T(8,128)S(1)...) custom-call(bf16[1536,768]{1,0:T(8,128)(2,1)} %get-tuple-element.43.q_ref, ...), custom_call_target="tpu_custom_call" | custom-call | flops 24159191040 | bytes 18874368 | tf_op jit(solution)/shard_map/pallas_call | solution.py:358
  261.8 0.0 copy-start.4
  261.8 1.4 copy-done.4
  263.3 9.9 %shard_map.208 = (bf16[1536,768]{1,0:T(8,128)(2,1)S(1)}, f32[1,768]{1,0:T(1,128)S(1)}) custom-call(bf16[1536,768]{1,0:T(8,128)(2,1)} %get-tuple-element.46.tok, f32[1,768]{1,0:T(1,128)S(1)} %reshape.79.gain, f32[1536,768]{1,0:T(8,128)} %get-tuple-element.64.gh, bf16[768,1536]{1,0:T(8,128)(2,1)} %copy-done.4, bf16[1536,768]{1,0:T(8,128)(2,1)} %get-tuple-element.62.dk.refs_4_, ...), custom_call_target="tpu_custom_call" | custom-call | flops 5435817984 | bytes 16777216 | tf_op jit(solution)/shard_map/pallas_call | solution.py:760
  273.2 0.0 copy-start.5
  273.2 1.4 copy-done.5
  274.6 0.1 reduce_sum.29
  274.8 0.1 copy.39
  274.9 0.1 reshape.76
  275.0 0.9 pad.10.refs_6_
  275.9 86.8 %shard_map.209 = (bf16[768,3584]{1,0:T(8,128)(2,1)}, bf16[12,128,768]{2,1,0:T(8,128)(2,1)}) custom-call(bf16[768,1536]{1,0:T(8,128)(2,1)} %get-tuple-element.59.refs_0_, bf16[1536,768]{1,0:T(8,128)(2,1)} %get-tuple-element.54.gb_ref.refs_1_, bf16[768,1536]{1,0:T(8,128)(2,1)} %get-tuple-element.60.refs_2_, bf16[768,1536]{1,0:T(8,128)(2,1)} %copy-done.4, ...), custom_call_target="tpu_custom_call" | custom-call | tf_op jit(solution)/shard_map/pallas_call | solution.py:1039
  362.8 1.0 slice_convert_fusion.4
  363.7 0.6 slice_bitcast_fusion
  364.3 0.1 reshape.78
  364.4 0.7 copy.40
  365.1 6.3 %slice_convert_fusion = (f32[768,768]{1,0:T(8,128)}, f32[768,768]{1,0:T(8,128)}, f32[768,768]{1,0:T(8,128)}, f32[768,768]{1,0:T(8,128)}) fusion(bf16[768,3584]{1,0:T(8,128)(2,1)} %get-tuple-element.70), kind=kLoop, calls=%fused_computation.2 | loop fusion | flops 2359296 | bytes 14155776 | tf_op jit(solution)/shard_map/convert_element_type | solution.py:1148
  371.5 5.0 %maximum_convert_fusion = f32[768,3072]{1,0:T(8,128)} fusion(bf16[768,1536]{1,0:T(8,128)(2,1)S(1)} %copy-done.20, bf16[768,1536]{1,0:T(8,128)(2,1)S(1)} %copy-done.18), kind=kLoop, calls=%fused_computation | loop fusion | flops 9437184 | bytes 14155776 | tf_op jit(solution)/shard_map/convert_element_type | solution.py:1146
  376.5 4.5 %maximum_convert_fusion.1 = f32[3072,768]{1,0:T(8,128)} fusion(bf16[1536,768]{1,0:T(8,128)(2,1)S(1)} %copy-done.19, bf16[1536,768]{1,0:T(8,128)(2,1)S(1)} %copy-done.17), kind=kLoop, calls=%fused_computation.1 | loop fusion | flops 9437184 | bytes 14155776 | tf_op jit(solution)/shard_map/convert_element_type | solution.py:1147
  381.0 1.4 copy.43
  382.4 1.1 copy-done.22
  383.5 1.4 copy.44
  (36 shorter events, 0.2 us)
Async XLA Ops:
  0.6 1.4 copy-start
  2.1 75.7 %copy-start.7 = (f32[1,768]{1,0:T(1,128)}, f32[1,768]{1,0:T(1,128)S(1)}, u32[]{:S(2)}) copy-start(f32[1,768]{1,0:T(1,128)S(1)} %reshape.80.gain) | copy-start | bytes 9220
  3.8 1.3 copy-start.10
  5.0 1.3 copy-start.12
  6.3 1.3 copy-start.14
  43.8 34.0 %copy-start.6 = (bf16[768,768]{1,0:T(8,128)(2,1)S(1)}, bf16[768,768]{1,0:T(8,128)(2,1)}, u32[]{:S(2)}) copy-start(bf16[768,768]{1,0:T(8,128)(2,1)} %wp_ref.1) | copy-start | bytes 3538948
  75.0 1.4 copy-start.2
  76.4 1.4 copy-start.3
  86.7 1.4 copy-start.8
  88.1 1.4 copy-start.9
  191.6 1.0 copy-start.16
  192.6 70.6 %copy-start.11 = (bf16[768,768]{1,0:T(8,128)(2,1)S(1)}, bf16[768,768]{1,0:T(8,128)(2,1)}, u32[]{:S(2)}) copy-start(bf16[768,768]{1,0:T(8,128)(2,1)} %wq.3) | copy-start | bytes 3538948
  192.6 70.6 %copy-start.13 = (bf16[768,768]{1,0:T(8,128)(2,1)S(1)}, bf16[768,768]{1,0:T(8,128)(2,1)}, u32[]{:S(2)}) copy-start(bf16[768,768]{1,0:T(8,128)(2,1)} %wk.3) | copy-start | bytes 3538948
  192.6 70.6 %copy-start.15 = (bf16[768,768]{1,0:T(8,128)(2,1)S(1)}, bf16[768,768]{1,0:T(8,128)(2,1)}, u32[]{:S(2)}) copy-start(bf16[768,768]{1,0:T(8,128)(2,1)} %wv.3) | copy-start | bytes 3538948
  261.8 1.4 copy-start.4
  263.2 11.3 %copy-start.23 = (f32[1,768]{1,0:T(1,128)S(1)}, f32[1,768]{1,0:T(1,128)}, u32[]{:S(2)}) copy-start(f32[1,768]{1,0:T(1,128)} %get-tuple-element.66) | copy-start | bytes 9220
  273.2 1.4 copy-start.5
  365.1 6.4 %copy-start.18 = (bf16[768,1536]{1,0:T(8,128)(2,1)S(1)}, bf16[768,1536]{1,0:T(8,128)(2,1)}, u32[]{:S(2)}) copy-start(bf16[768,1536]{1,0:T(8,128)(2,1)} %get-tuple-element.71) | copy-start | bytes 7077892
  365.1 6.4 %copy-start.20 = (bf16[768,1536]{1,0:T(8,128)(2,1)S(1)}, bf16[768,1536]{1,0:T(8,128)(2,1)}, u32[]{:S(2)}) copy-start(bf16[768,1536]{1,0:T(8,128)(2,1)} %get-tuple-element.72) | copy-start | bytes 7077892
  371.5 5.0 %copy-start.17 = (bf16[1536,768]{1,0:T(8,128)(2,1)S(1)}, bf16[1536,768]{1,0:T(8,128)(2,1)}, u32[]{:S(2)}) copy-start(bf16[1536,768]{1,0:T(8,128)(2,1)} %get-tuple-element.73) | copy-start | bytes 7077892
  371.5 5.0 %copy-start.19 = (bf16[1536,768]{1,0:T(8,128)(2,1)S(1)}, bf16[1536,768]{1,0:T(8,128)(2,1)}, u32[]{:S(2)}) copy-start(bf16[1536,768]{1,0:T(8,128)(2,1)} %get-tuple-element.74) | copy-start | bytes 7077892
  376.5 4.5 %copy-start.21 = (bf16[12,128,768]{2,1,0:T(8,128)(2,1)S(1)}, bf16[12,128,768]{2,1,0:T(8,128)(2,1)}, u32[]{:S(2)}) copy-start(bf16[12,128,768]{2,1,0:T(8,128)(2,1)} %get-tuple-element.149) | copy-start | bytes 7077892
  381.0 2.5 copy-start.22
  381.0 3.9 %copy-start.1 = (s32[12,6]{0,1:T(8,128)S(1)}, s32[12,6]{0,1:T(8,128)}, u32[]{:S(2)}) copy-start(s32[12,6]{0,1:T(8,128)} %param.13) | copy-start | bytes 868
where the time goes:
time: 386 us; the launch traced here: 385 us
  Pallas kernels  344 us (89%)
  local copies, waits for them, and re-layouts  22 us (6%)
  other arithmetic  17.7 us (5%)
    pallas_call x1, Pallas kernels, ffn_summed(): pl.pallas_call(functools.partial(ffn_kernel, depth, scale), in_specs=[vm]...  102 us
    pallas_call x1, Pallas kernels, rest_summed(): pl.pallas_call(functools.partial(rest_kernel, depth, scale), in_specs=[an...  86.8 us
    pallas_call x1, Pallas kernels, attend_back(): pl.pallas_call(functools.partial(attend_back_kernel, depth), grid=(pairs,...  69.2 us
    pallas_call x3, Pallas kernels, plain_call(): pl.pallas_call(kernel, grid=(count // TOK,), in_specs=in_specs, out_specs...  55 us
    pallas_call x1, Pallas kernels, attend(): pl.pallas_call(attend_kernel, grid=(pairs, row_count), in_specs=[rows, ro...  31.2 us
    unnamed x51, local copies, waits for them, and re-layouts  17.8 us

commit v1 on v0

--- a/solution.py
+++ b/solution.py
@@ -974,14 +974,14 @@
 
 
 def rest_kernel(depth, scale, *refs):
-    sources, (small, done, out, out_ref) = refs[:6], refs[6:10]
-    mix, gb, normed_flat, dq, dk, dv = held = refs[10:16]
-    load_sem, share, *refs = refs[16:]
+    sources, (small, gain, out, out_ref) = refs[:11], refs[11:15]
+    mix, gb, normed_flat, dq, dk, dv, tok, gh, wq, wk, wv = held = refs[15:26]
+    done, gain_sum, load_sem, share, *refs = refs[26:]
     width = normed_flat.shape[0]
     each = width // CH_COLS
     chunks = share.shape[0]
     loads = [pltpu.make_async_copy(a, b, load_sem.at[i]) for i, (a, b) in enumerate(zip(sources, held))]
-    needs = (loads[:2], loads[2:4], loads[4:5], loads[5:])
+    gain_sum[...] = jnp.zeros_like(gain_sum)
     for d in loads:
         d.start()
     swap = Exchange(done, out_ref, *refs[:3], False, SWAPS)
@@ -995,32 +995,55 @@
             return dot(normed_flat[...], dq[cut], 1, 1)
         return dot(normed_flat[...], (dk if which == 2 else dv)[:, cut], 1, 0)
 
+    def tokens_back(m):
+        rows = spans(m * TOK, TOK, TOK)
+        wide = tok[rows].astype(F32)
+        _, inverse = apply_rms_scaling(wide, gain[...])
+        grad_normed = (
+            dot(dq[:, rows].T, wq[...], 1, 1) + dot(dk[rows], wk[...], 1, 1) + dot(dv[rows], wv[...], 1, 1)
+        )
+        part, grad_gain = norm_back(wide, inverse, gain[...], grad_normed)
+        done[m] = (gh[rows] + part).astype(BF)
+        gain_sum[...] += grad_gain[None]
+        each_row = SWAPS // done.shape[0]
+        for i in range(each_row):
+            swap.start(m * each_row + i)
+
     def step(p, _):
+        @pl.when(p == 0)
+        def _():
+            for d in loads[:2]:
+                d.wait()
+
+        @pl.when(p == 1)
+        def _():
+            for d in loads[2:]:
+                d.wait()
+
         for kind in range(2):
             c = 2 * p + kind
             for which in range(4):
 
                 @pl.when(c // each == which)
                 def _():
-                    @pl.when(c == which * each)
-                    def _():
-                        for d in needs[which]:
-                            d.wait()
-
                     cut = spans((c - which * each) * CH_COLS, CH_COLS, CH_COLS)
                     summing.put(c, terms(which, cut))
 
             @pl.when(c >= 4 * each)
             def _():
-                summing.put(c, small[:, spans((c - 4 * each) * CH_COLS, CH_COLS, CH_COLS)])
-
-        for i in range(2):
-
-            @pl.when(2 * p + i < SWAPS)
-            def _():
-                swap.start(2 * p + i)
+                value = small[:, spans((c - 4 * each) * CH_COLS, CH_COLS, CH_COLS)]
+                lines = width // BLK
+                first = [gain_sum[:, i * BLK : (i + 1) * BLK] for i in range(lines)]
+                first.append(jnp.zeros((CH_ROWS - lines, BLK), F32))
+                first = jnp.concatenate([jnp.concatenate(first, axis=0), jnp.zeros((CH_ROWS, BLK), F32)], axis=1)
+                summing.put(c, value.astype(F32) + jnp.where(c == 4 * each, first, 0.0))
 
         summing.tick(p, BOTH_STEPS, REST_LAG)
+
+        @pl.when((p >= 1) & (p <= done.shape[0]))
+        def _():
+            tokens_back(p - 1)
+
         return 0
 
     lax.fori_loop(0, chunks // 2, step, 0)
@@ -1029,29 +1052,30 @@
     swap.finish()
 
 
-def rest_summed(normed_flat, dq, dk, dv, mix, gb, small, done, scale, depth):
+def rest_summed(normed_flat, dq, dk, dv, mix, gb, tok, gh, wq, wk, wv, gain, small, mine, scale, depth):
     width, count = normed_flat.shape
     chunks = (4 * width + small.shape[1]) // CH_COLS
     vm = pl.BlockSpec(memory_space=pltpu.VMEM)
     anywhere = pl.BlockSpec(memory_space=pl.ANY)
-    mine, row_len, _ = done.shape
-    sources = (mix, gb, normed_flat, dq, dk, dv)
+    row_len = count // mine
+    sources = (mix, gb, normed_flat, dq, dk, dv, tok, gh, wq, wk, wv)
     return pl.pallas_call(
         functools.partial(rest_kernel, depth, scale),
-        in_specs=[anywhere] * 6 + [vm, anywhere],
+        in_specs=[anywhere] * len(sources) + [vm, vm],
         out_specs=[anywhere] * 2,
         out_shape=[
             jax.ShapeDtypeStruct((CH_ROWS, chunks * CH_COLS), BF),
             jax.ShapeDtypeStruct((mine * SEQ, row_len // SEQ, width), BF),
         ],
-        scratch_shapes=[pltpu.VMEM(a.shape, BF) for a in sources]
-        + [pltpu.SemaphoreType.DMA((6,)), pltpu.VMEM(Summing.share_shape(chunks, depth), BF)]
+        scratch_shapes=[pltpu.VMEM(a.shape, a.dtype) for a in sources]
+        + [pltpu.VMEM((mine, row_len, width), BF), pltpu.VMEM((1, width), F32)]
+        + [pltpu.SemaphoreType.DMA((len(sources),)), pltpu.VMEM(Summing.share_shape(chunks, depth), BF)]
         + Exchange.scratch(SWAPS)
         + Summing.sum_scratch(chunks, depth)
         + Summing.give_scratch(chunks, depth, False),
         compiler_params=pltpu.CompilerParams(
             collective_id=2, has_side_effects=True, vmem_limit_bytes=60 << 20),
-    )(*sources, small, done)
+    )(*sources, small, gain)
 
 
 def reduce_plain(flat, scale):
@@ -1130,17 +1154,20 @@
     dq_flat, dk_rows, dv_rows, table, *given = attend_back(
         q_rows, k_rows, v_rows, w_output, branch, mix, stat, fq, fk, bias, row_len, gives
     )
-    grad_input, sum_one = after(
-        tok, gain_one, grad_hidden, dq_flat, dk_rows, dv_rows, w_query, w_key, w_value
-    )
+    if fused:
+        sum_one = jnp.zeros((1, width), F32)
+    else:
+        grad_input, sum_one = after(
+            tok, gain_one, grad_hidden, dq_flat, dk_rows, dv_rows, w_query, w_key, w_value
+        )
     sum_table = jnp.sum(table, axis=2).T
     small = jnp.concatenate([sum_one.reshape(-1), sum_two.reshape(-1), sum_table.reshape(-1)])
     if fused:
         small = jnp.pad(small, (0, -small.size % (CH_ROWS * BLK))).reshape(CH_ROWS, BLK)
         small = jnp.pad(small.astype(BF), ((0, 0), (0, 2 * CH_COLS - BLK)))
         total, grad_back = rest_summed(
-            normed_flat, dq_flat, dk_rows, dv_rows, mix_flat, branch, small,
-            grad_input.reshape(mine, row_len, width), scale, depth,
+            normed_flat, dq_flat, dk_rows, dv_rows, mix_flat, branch, tok, grad_hidden,
+            w_query, w_key, w_value, gain_one, small, mine, scale, depth,
         )
         out_back = given[2]
         grad_inner = jnp.concatenate([early[0], given[0]], axis=1).astype(F32)

time: 386 us -> 384 us (level)
    pallas_call x3 -> x2, Pallas kernels: 55 us -> 45 us  [plain_call(): pl.pallas_call(kernel, grid=(count // TOK,), in_specs=in_specs, out_specs...]
    pallas_call x1, Pallas kernels: 86.8 us -> 95.8 us  [rest_summed(): pl.pallas_call(functools.partial(rest_kernel, depth, scale), in_specs=[an...]
    unnamed x51 -> x45, local copies, waits for them, and re-layouts: 17.8 us -> 15.7 us
where the time goes in v1:
time: 384 us
  Pallas kernels  343 us (89%)
  other arithmetic  20.3 us (5%)
  local copies, waits for them, and re-layouts  19.2 us (5%)
    pallas_call x1, Pallas kernels, ffn_summed(): pl.pallas_call(functools.partial(ffn_kernel, depth, scale), in_specs=[vm]...  102 us
    pallas_call x1, Pallas kernels, rest_summed(): pl.pallas_call(functools.partial(rest_kernel, depth, scale), in_specs=[an...  95.8 us
    pallas_call x1, Pallas kernels, attend_back(): pl.pallas_call(functools.partial(attend_back_kernel, depth), grid=(pairs,...  69.5 us
    pallas_call x2, Pallas kernels, plain_call(): pl.pallas_call(kernel, grid=(count // TOK,), in_specs=in_specs, out_specs...  45 us
    pallas_call x1, Pallas kernels, attend(): pl.pallas_call(attend_kernel, grid=(pairs, row_count), in_specs=[rows, ro...  31.3 us
    unnamed x45, local copies, waits for them, and re-layouts  15.7 us

profile of v1, /device:TPU:1, one launch (start us, length us, event | category | flops | bytes accessed | tf_op | source)
XLA Modules:
  0.0 383.7 jit_solution(11146198672419005135)
XLA Ops:
  0.6 0.0 copy-start
  0.7 0.7 copy-done
  1.3 0.1 constant_dynamic-slice_fusion
  1.4 0.1 copy.38
  1.5 0.1 select_reduce_fusion
  1.6 0.1 convert_reduce_fusion
  1.7 0.3 select_convert_fusion
  2.0 0.2 pad_maximum_fusion.fk_ref
  2.3 0.7 reshape.74.gain.refs_12_
  3.0 0.8 copy.37.table
  3.7 1.3 copy-done.6
  5.0 1.3 copy-done.7
  6.3 1.3 copy-done.8
  7.6 36.1 %shard_map.203 = (bf16[1536,768]{1,0:T(8,128)(2,1)}, bf16[768,1536]{1,0:T(8,128)(2,1)}, bf16[1536,768]{1,0:T(8,128)(2,1)}, bf16[1536,768]{1,0:T(8,128)(2,1)}, bf...) custom-call(bf16[12,128,768]{2,1,0:T(8,128)(2,1)} %tok.1, ...), custom_call_target="tpu_custom_call" | custom-call | flops 5435817984 | bytes 16777216 | tf_op jit(solution)/shard_map/pallas_call | solution.py:760
  43.6 0.0 copy-done.10
  43.6 0.0 copy-start.20
  43.7 0.0 copy-start.5
  43.7 31.3 %shard_map.204 = (bf16[1536,768]{1,0:T(8,128)(2,1)S(1)}, f32[3,6,2,512]{3,2,1,0:T(2,128)S(1)}, bf16[3,512,768]{2,1,0:T(8,128)(2,1)S(1)}) custom-call(bf16[1536,768]{1,0:T(8,128)(2,1)} %get-tuple-element.41.q_ref, bf16[1536,768]{1,0:T(8,128)(2,1)} %get-tuple-element.42.k_ref, bf16[1536,768]{1,0:T(8,128)(2,1)} %get-tuple-element.43.v_ref, ...), custom_call_target="tpu_custom_call" | custom-call | flops 9663676416 | bytes 9437184 | tf_op jit(solution)/shard_map/pallas_call | solution.py:324
  75.0 0.0 copy-start.2
  75.0 1.4 copy-done.2
  76.4 1.4 copy-done.3
  77.8 0.0 copy-start.9
  77.8 8.9 %shard_map.205 = (f32[1536,768]{1,0:T(8,128)}, bf16[1536,768]{1,0:T(8,128)(2,1)S(1)}, bf16[768,1536]{1,0:T(8,128)(2,1)S(1)}, bf16[768,1536]{1,0:T(8,128)(2,1)}, bf16[768,1536]{1,0:T(8,128)(2,1)}) custom-call(bf16[1536,768]{1,0:T(8,128)(2,1)} %get-tuple-element.44.tok.refs_6_, bf16[1536,768]{1,0:T(8,128)(2,1)} %copy-done.2, bf16[768,768]{1,0:T(8,128)(2,1)S(1)} %copy-done.5, ...), custom_call_target="tpu_custom_call" | custom-call | flops 1811939328 | bytes 16777216 | tf_op jit(solution)/shard_map/pallas_call | solution.py:760
  86.7 0.0 copy-done.9
  86.7 1.4 copy-done.11
  88.1 1.4 copy-done.12
  89.5 101.8 %shard_map.206 = (bf16[1536,768]{1,0:T(8,128)(2,1)}, f32[1536,768]{1,0:T(8,128)}, bf16[1536,768]{1,0:T(8,128)(2,1)}, f32[1,768]{1,0:T(1,128)}, bf16[24,48,128]{2...) custom-call(bf16[1536,768]{1,0:T(8,128)(2,1)} %copy-done.11, bf16[768,1536]{1,0:T(8,128)(2,1)} %copy-done.12, ...), custom_call_target="tpu_custom_call" | custom-call | flops 43486543872 | bytes 41943040 | tf_op jit(solution)/shard_map/pallas_call | solution.py:943
  191.3 1.0 copy-done.13
  192.3 69.5 %shard_map.207 = (bf16[768,1536]{1,0:T(8,128)(2,1)S(1)}, bf16[1536,768]{1,0:T(8,128)(2,1)}, bf16[1536,768]{1,0:T(8,128)(2,1)}, f32[12,32,128]{2,1,0:T(8,128)S(1)...) custom-call(bf16[1536,768]{1,0:T(8,128)(2,1)} %get-tuple-element.41.q_ref, ...), custom_call_target="tpu_custom_call" | custom-call | flops 24159191040 | bytes 18874368 | tf_op jit(solution)/shard_map/pallas_call | solution.py:358
  261.7 0.0 copy-start.4
  261.7 0.0 copy-done.15
  261.8 0.0 copy-start.14
  261.8 0.0 copy-start.16
  261.8 7.0 %maximum_convert_fusion.1 = f32[3072,768]{1,0:T(8,128)} fusion(bf16[1536,768]{1,0:T(8,128)(2,1)} %get-tuple-element.70, bf16[1536,768]{1,0:T(8,128)(2,1)S(1)} %copy-done.15), kind=kLoop, calls=%fused_computation.1 | loop fusion | flops 9437184 | bytes 14155776 | tf_op jit(solution)/shard_map/convert_element_type | solution.py:1174
  268.8 5.0 %maximum_convert_fusion = f32[768,3072]{1,0:T(8,128)} fusion(bf16[768,1536]{1,0:T(8,128)(2,1)S(1)} %copy-done.16, bf16[768,1536]{1,0:T(8,128)(2,1)S(1)} %copy-done.14), kind=kLoop, calls=%fused_computation | loop fusion | flops 9437184 | bytes 14155776 | tf_op jit(solution)/shard_map/convert_element_type | solution.py:1173
  273.9 0.1 reduce_sum.29
  274.0 0.1 copy.39
  274.1 0.1 reshape.72
  274.3 0.9 pad.10.refs_11_
  275.2 95.8 %shard_map.208 = (bf16[768,3584]{1,0:T(8,128)(2,1)}, bf16[12,128,768]{2,1,0:T(8,128)(2,1)}) custom-call(bf16[768,1536]{1,0:T(8,128)(2,1)} %get-tuple-element.57.refs_0_, bf16[1536,768]{1,0:T(8,128)(2,1)} %get-tuple-element.52.gb_ref.refs_1_, bf16[768,1536]{1,0:T(8,128)(2,1)} %get-tuple-element.58.refs_2_, bf16[768,1536]{1,0:T(8,128)(2,1)} %copy-done.4, ...), custom_call_target="tpu_custom_call" | custom-call | tf_op jit(solution)/shard_map/pallas_call | solution.py:1062
  371.0 6.3 %slice_convert_fusion = (f32[768,768]{1,0:T(8,128)}, f32[768,768]{1,0:T(8,128)}, f32[768,768]{1,0:T(8,128)}, f32[768,768]{1,0:T(8,128)}) fusion(bf16[768,3584]{1,0:T(8,128)(2,1)} %get-tuple-element.66), kind=kLoop, calls=%fused_computation.2 | loop fusion | flops 2359296 | bytes 14155776 | tf_op jit(solution)/shard_map/convert_element_type | solution.py:1175
  377.4 1.0 slice_convert_fusion.4
  378.3 0.1 reshape.73
  378.4 0.7 copy.40
  379.1 0.6 slice_bitcast_fusion
  379.7 1.4 copy.43
  381.1 1.1 copy-done.18
  382.2 1.4 copy.44
  (30 shorter events, 0.1 us)
Async XLA Ops:
  0.6 0.7 copy-start
  3.0 40.7 %copy-start.10 = (f32[1,768]{1,0:T(1,128)}, f32[1,768]{1,0:T(1,128)S(1)}, u32[]{:S(2)}) copy-start(f32[1,768]{1,0:T(1,128)S(1)} %reshape.74.gain.refs_12_) | copy-start | bytes 9220
  3.7 1.3 copy-start.6
  5.0 1.3 copy-start.7
  6.3 1.3 copy-start.8
  43.6 34.2 %copy-start.20 = (bf16[768]{0:T(1024)(128)(2,1)S(1)}, bf16[768]{0:T(1024)(128)(2,1)}, u32[]{:S(2)}) copy-start(bf16[768]{0:T(1024)(128)(2,1)} %param.21) | copy-start | bytes 4612
  43.7 34.2 %copy-start.5 = (bf16[768,768]{1,0:T(8,128)(2,1)S(1)}, bf16[768,768]{1,0:T(8,128)(2,1)}, u32[]{:S(2)}) copy-start(bf16[768,768]{1,0:T(8,128)(2,1)} %wp_ref.1) | copy-start | bytes 3538948
  75.0 1.4 copy-start.2
  76.4 1.4 copy-start.3
  77.8 8.9 %copy-start.9 = (f32[1,768]{1,0:T(1,128)}, f32[1,768]{1,0:T(1,128)S(1)}, u32[]{:S(2)}) copy-start(f32[1,768]{1,0:T(1,128)S(1)} %reshape.75.gain) | copy-start | bytes 9220
  86.7 1.4 copy-start.11
  88.1 1.4 copy-start.12
  191.3 1.0 copy-start.13
  192.3 69.5 %copy-start.15 = (bf16[1536,768]{1,0:T(8,128)(2,1)S(1)}, bf16[1536,768]{1,0:T(8,128)(2,1)}, u32[]{:S(2)}) copy-start(bf16[1536,768]{1,0:T(8,128)(2,1)} %get-tuple-element.69) | copy-start | bytes 7077892
  261.7 7.1 %copy-start.4 = (bf16[768,1536]{1,0:T(8,128)(2,1)}, bf16[768,1536]{1,0:T(8,128)(2,1)S(1)}, u32[]{:S(2)}) copy-start(bf16[768,1536]{1,0:T(8,128)(2,1)S(1)} %get-tuple-element.59.refs_3_) | copy-start | bytes 7077892
  261.8 7.1 %copy-start.14 = (bf16[768,1536]{1,0:T(8,128)(2,1)S(1)}, bf16[768,1536]{1,0:T(8,128)(2,1)}, u32[]{:S(2)}) copy-start(bf16[768,1536]{1,0:T(8,128)(2,1)} %get-tuple-element.67) | copy-start | bytes 7077892
  261.8 7.0 %copy-start.16 = (bf16[768,1536]{1,0:T(8,128)(2,1)S(1)}, bf16[768,1536]{1,0:T(8,128)(2,1)}, u32[]{:S(2)}) copy-start(bf16[768,1536]{1,0:T(8,128)(2,1)} %get-tuple-element.68) | copy-start | bytes 7077892
  268.8 5.4 %copy-start.19 = (f32[1,768]{1,0:T(1,128)S(1)}, f32[1,768]{1,0:T(1,128)}, u32[]{:S(2)}) copy-start(f32[1,768]{1,0:T(1,128)} %get-tuple-element.63) | copy-start | bytes 9220
  371.0 8.7 %copy-start.17 = (bf16[12,128,768]{2,1,0:T(8,128)(2,1)S(1)}, bf16[12,128,768]{2,1,0:T(8,128)(2,1)}, u32[]{:S(2)}) copy-start(bf16[12,128,768]{2,1,0:T(8,128)(2,1)} %get-tuple-element.143) | copy-start | bytes 7077892
  379.7 2.5 copy-start.18
  379.7 3.9 %copy-start.1 = (s32[12,6]{0,1:T(8,128)S(1)}, s32[12,6]{0,1:T(8,128)}, u32[]{:S(2)}) copy-start(s32[12,6]{0,1:T(8,128)} %param.13) | copy-start | bytes 868

commit v2 on v1

--- a/solution.py
+++ b/solution.py
@@ -27,7 +27,7 @@
 CH_ROWS, CH_COLS = 768, 256
 SUM_STEPS = ((1,), (2,), (3,), (4,))
 GIVE_STEPS = ((5,), (6,), (7,), (8,), (9,))
-GIVE_LAG = 3
+GIVE_LAG = 4
 EARLY = 6
 SWAPS = 12
 SEQ = 4

time: 384 us -> 378 us (0.984)
  Pallas kernels: 343 us -> 337 us
    pallas_call x1, Pallas kernels: 69.5 us -> 64.4 us  [attend_back(): pl.pallas_call(functools.partial(attend_back_kernel, depth), grid=(pairs,...]
where the time goes in v2:
time: 378 us
  Pallas kernels  337 us (89%)
  other arithmetic  20.3 us (5%)
  local copies, waits for them, and re-layouts  19.2 us (5%)
    pallas_call x1, Pallas kernels, ffn_summed(): pl.pallas_call(functools.partial(ffn_kernel, depth, scale), in_specs=[vm]...  102 us
    pallas_call x1, Pallas kernels, rest_summed(): pl.pallas_call(functools.partial(rest_kernel, depth, scale), in_specs=[an...  94.8 us
    pallas_call x1, Pallas kernels, attend_back(): pl.pallas_call(functools.partial(attend_back_kernel, depth), grid=(pairs,...  64.4 us
    pallas_call x2, Pallas kernels, plain_call(): pl.pallas_call(kernel, grid=(count // TOK,), in_specs=in_specs, out_specs...  45 us
    pallas_call x1, Pallas kernels, attend(): pl.pallas_call(attend_kernel, grid=(pairs, row_count), in_specs=[rows, ro...  31.3 us
    unnamed x45, local copies, waits for them, and re-layouts  15.7 us

profile of v2, /device:TPU:1, one launch (start us, length us, event | category | flops | bytes accessed | tf_op | source)
XLA Modules:
  0.0 377.6 jit_solution(10370520336126906167)
XLA Ops:
  0.6 0.0 copy-start
  0.7 0.7 copy-done
  1.3 0.1 constant_dynamic-slice_fusion
  1.4 0.1 copy.38
  1.5 0.1 select_reduce_fusion
  1.6 0.1 convert_reduce_fusion
  1.7 0.3 select_convert_fusion
  2.0 0.2 pad_maximum_fusion.fk_ref
  2.3 0.7 reshape.74.gain.refs_12_
  3.0 0.8 copy.37.table
  3.7 1.3 copy-done.6
  5.0 1.3 copy-done.7
  6.3 1.3 copy-done.8
  7.6 36.1 %shard_map.203 = (bf16[1536,768]{1,0:T(8,128)(2,1)}, bf16[768,1536]{1,0:T(8,128)(2,1)}, bf16[1536,768]{1,0:T(8,128)(2,1)}, bf16[1536,768]{1,0:T(8,128)(2,1)}, bf...) custom-call(bf16[12,128,768]{2,1,0:T(8,128)(2,1)} %tok.1, ...), custom_call_target="tpu_custom_call" | custom-call | flops 5435817984 | bytes 16777216 | tf_op jit(solution)/shard_map/pallas_call | solution.py:760
  43.6 0.0 copy-done.10
  43.6 0.0 copy-start.20
  43.7 0.0 copy-start.5
  43.7 31.3 %shard_map.204 = (bf16[1536,768]{1,0:T(8,128)(2,1)S(1)}, f32[3,6,2,512]{3,2,1,0:T(2,128)S(1)}, bf16[3,512,768]{2,1,0:T(8,128)(2,1)S(1)}) custom-call(bf16[1536,768]{1,0:T(8,128)(2,1)} %get-tuple-element.41.q_ref, bf16[1536,768]{1,0:T(8,128)(2,1)} %get-tuple-element.42.k_ref, bf16[1536,768]{1,0:T(8,128)(2,1)} %get-tuple-element.43.v_ref, ...), custom_call_target="tpu_custom_call" | custom-call | flops 9663676416 | bytes 9437184 | tf_op jit(solution)/shard_map/pallas_call | solution.py:324
  75.0 0.0 copy-start.2
  75.0 1.4 copy-done.2
  76.4 1.4 copy-done.3
  77.8 0.0 copy-done.20
  77.8 0.0 copy-done.5
  77.8 0.0 copy-start.9
  77.8 8.9 %shard_map.205 = (f32[1536,768]{1,0:T(8,128)}, bf16[1536,768]{1,0:T(8,128)(2,1)S(1)}, bf16[768,1536]{1,0:T(8,128)(2,1)S(1)}, bf16[768,1536]{1,0:T(8,128)(2,1)}, bf16[768,1536]{1,0:T(8,128)(2,1)}) custom-call(bf16[1536,768]{1,0:T(8,128)(2,1)} %get-tuple-element.44.tok.refs_6_, bf16[1536,768]{1,0:T(8,128)(2,1)} %copy-done.2, bf16[768,768]{1,0:T(8,128)(2,1)S(1)} %copy-done.5, ...), custom_call_target="tpu_custom_call" | custom-call | flops 1811939328 | bytes 16777216 | tf_op jit(solution)/shard_map/pallas_call | solution.py:760
  86.7 1.4 copy-done.11
  88.1 1.4 copy-done.12
  89.5 101.8 %shard_map.206 = (bf16[1536,768]{1,0:T(8,128)(2,1)}, f32[1536,768]{1,0:T(8,128)}, bf16[1536,768]{1,0:T(8,128)(2,1)}, f32[1,768]{1,0:T(1,128)}, bf16[24,48,128]{2...) custom-call(bf16[1536,768]{1,0:T(8,128)(2,1)} %copy-done.11, bf16[768,1536]{1,0:T(8,128)(2,1)} %copy-done.12, ...), custom_call_target="tpu_custom_call" | custom-call | flops 43486543872 | bytes 41943040 | tf_op jit(solution)/shard_map/pallas_call | solution.py:943
  191.3 0.0 copy-start.13
  191.3 1.0 copy-done.13
  192.3 64.4 %shard_map.207 = (bf16[768,1536]{1,0:T(8,128)(2,1)S(1)}, bf16[1536,768]{1,0:T(8,128)(2,1)}, bf16[1536,768]{1,0:T(8,128)(2,1)}, f32[12,32,128]{2,1,0:T(8,128)S(1)...) custom-call(bf16[1536,768]{1,0:T(8,128)(2,1)} %get-tuple-element.41.q_ref, ...), custom_call_target="tpu_custom_call" | custom-call | flops 24159191040 | bytes 18874368 | tf_op jit(solution)/shard_map/pallas_call | solution.py:358
  256.7 0.0 copy-start.4
  256.7 7.0 %maximum_convert_fusion.1 = f32[3072,768]{1,0:T(8,128)} fusion(bf16[1536,768]{1,0:T(8,128)(2,1)} %get-tuple-element.70, bf16[1536,768]{1,0:T(8,128)(2,1)S(1)} %copy-done.15), kind=kLoop, calls=%fused_computation.1 | loop fusion | flops 9437184 | bytes 14155776 | tf_op jit(solution)/shard_map/convert_element_type | solution.py:1174
  263.8 5.0 %maximum_convert_fusion = f32[768,3072]{1,0:T(8,128)} fusion(bf16[768,1536]{1,0:T(8,128)(2,1)S(1)} %copy-done.16, bf16[768,1536]{1,0:T(8,128)(2,1)S(1)} %copy-done.14), kind=kLoop, calls=%fused_computation | loop fusion | flops 9437184 | bytes 14155776 | tf_op jit(solution)/shard_map/convert_element_type | solution.py:1173
  268.8 0.1 reduce_sum.29
  268.9 0.1 copy.39
  269.0 0.1 reshape.72
  269.2 0.0 copy-done.19
  269.2 0.9 pad.10.refs_11_
  270.2 94.8 %shard_map.208 = (bf16[768,3584]{1,0:T(8,128)(2,1)}, bf16[12,128,768]{2,1,0:T(8,128)(2,1)}) custom-call(bf16[768,1536]{1,0:T(8,128)(2,1)} %get-tuple-element.57.refs_0_, bf16[1536,768]{1,0:T(8,128)(2,1)} %get-tuple-element.52.gb_ref.refs_1_, bf16[768,1536]{1,0:T(8,128)(2,1)} %get-tuple-element.58.refs_2_, bf16[768,1536]{1,0:T(8,128)(2,1)} %copy-done.4, ...), custom_call_target="tpu_custom_call" | custom-call | tf_op jit(solution)/shard_map/pallas_call | solution.py:1062
  365.0 6.3 %slice_convert_fusion = (f32[768,768]{1,0:T(8,128)}, f32[768,768]{1,0:T(8,128)}, f32[768,768]{1,0:T(8,128)}, f32[768,768]{1,0:T(8,128)}) fusion(bf16[768,3584]{1,0:T(8,128)(2,1)} %get-tuple-element.66), kind=kLoop, calls=%fused_computation.2 | loop fusion | flops 2359296 | bytes 14155776 | tf_op jit(solution)/shard_map/convert_element_type | solution.py:1175
  371.3 1.0 slice_convert_fusion.4
  372.3 0.1 reshape.73
  372.4 0.7 copy.40
  373.1 0.6 slice_bitcast_fusion
  373.7 1.4 copy.43
  375.1 1.1 copy-done.18
  376.2 1.4 copy.44
  (30 shorter events, 0.1 us)
Async XLA Ops:
  0.6 0.7 copy-start
  3.0 40.7 %copy-start.10 = (f32[1,768]{1,0:T(1,128)}, f32[1,768]{1,0:T(1,128)S(1)}, u32[]{:S(2)}) copy-start(f32[1,768]{1,0:T(1,128)S(1)} %reshape.74.gain.refs_12_) | copy-start | bytes 9220
  3.7 1.3 copy-start.6
  5.0 1.3 copy-start.7
  6.3 1.3 copy-start.8
  43.6 34.2 %copy-start.20 = (bf16[768]{0:T(1024)(128)(2,1)S(1)}, bf16[768]{0:T(1024)(128)(2,1)}, u32[]{:S(2)}) copy-start(bf16[768]{0:T(1024)(128)(2,1)} %param.21) | copy-start | bytes 4612
  43.7 34.2 %copy-start.5 = (bf16[768,768]{1,0:T(8,128)(2,1)S(1)}, bf16[768,768]{1,0:T(8,128)(2,1)}, u32[]{:S(2)}) copy-start(bf16[768,768]{1,0:T(8,128)(2,1)} %wp_ref.1) | copy-start | bytes 3538948
  75.0 1.4 copy-start.2
  76.4 1.4 copy-start.3
  77.8 8.9 %copy-start.9 = (f32[1,768]{1,0:T(1,128)}, f32[1,768]{1,0:T(1,128)S(1)}, u32[]{:S(2)}) copy-start(f32[1,768]{1,0:T(1,128)S(1)} %reshape.75.gain) | copy-start | bytes 9220
  86.7 1.4 copy-start.11
  88.1 1.4 copy-start.12
  191.3 1.0 copy-start.13
  192.3 64.5 %copy-start.15 = (bf16[1536,768]{1,0:T(8,128)(2,1)S(1)}, bf16[1536,768]{1,0:T(8,128)(2,1)}, u32[]{:S(2)}) copy-start(bf16[1536,768]{1,0:T(8,128)(2,1)} %get-tuple-element.69) | copy-start | bytes 7077892
  256.7 7.1 %copy-start.4 = (bf16[768,1536]{1,0:T(8,128)(2,1)}, bf16[768,1536]{1,0:T(8,128)(2,1)S(1)}, u32[]{:S(2)}) copy-start(bf16[768,1536]{1,0:T(8,128)(2,1)S(1)} %get-tuple-element.59.refs_3_) | copy-start | bytes 7077892
  256.7 7.1 %copy-start.14 = (bf16[768,1536]{1,0:T(8,128)(2,1)S(1)}, bf16[768,1536]{1,0:T(8,128)(2,1)}, u32[]{:S(2)}) copy-start(bf16[768,1536]{1,0:T(8,128)(2,1)} %get-tuple-element.67) | copy-start | bytes 7077892
  256.7 7.0 %copy-start.16 = (bf16[768,1536]{1,0:T(8,128)(2,1)S(1)}, bf16[768,1536]{1,0:T(8,128)(2,1)}, u32[]{:S(2)}) copy-start(bf16[768,1536]{1,0:T(8,128)(2,1)} %get-tuple-element.68) | copy-start | bytes 7077892
  263.8 5.4 %copy-start.19 = (f32[1,768]{1,0:T(1,128)S(1)}, f32[1,768]{1,0:T(1,128)}, u32[]{:S(2)}) copy-start(f32[1,768]{1,0:T(1,128)} %get-tuple-element.63) | copy-start | bytes 9220
  365.0 8.7 %copy-start.17 = (bf16[12,128,768]{2,1,0:T(8,128)(2,1)S(1)}, bf16[12,128,768]{2,1,0:T(8,128)(2,1)}, u32[]{:S(2)}) copy-start(bf16[12,128,768]{2,1,0:T(8,128)(2,1)} %get-tuple-element.143) | copy-start | bytes 7077892
  373.7 2.5 copy-start.18
  373.7 3.9 %copy-start.1 = (s32[12,6]{0,1:T(8,128)S(1)}, s32[12,6]{0,1:T(8,128)}, u32[]{:S(2)}) copy-start(s32[12,6]{0,1:T(8,128)} %param.13) | copy-start | bytes 868
